TPU v7x, 768 devices: a whole 4x8x12 slice. The times are simulated.
768 devices in a mesh: gx: 4 (over x), yz: 192 (over z, y, core).
Axes of the slice: x: 4, y: 8, z: 12, core: 2. Of those that a mesh axis runs over, the one named last changes fastest.
Arguments:
- tokens: bfloat16 [384, 12288], P('yz', 'gx'), may hold values from -6 to 6
- counts: int32 [48], replicated, may hold values from 1 to 8, 192 in all
- gate_weight: bfloat16 [12288, 49152], P('gx', 'yz'), may hold values from -0.0546875 to 0.0546875
- up_weight: bfloat16 [12288, 49152], P('gx', 'yz'), may hold values from -0.0546875 to 0.0546875
- down_weight: bfloat16 [49152, 12288], P('yz', 'gx'), may hold values from -0.02734375 to 0.02734375
Outputs:
- mixed: bfloat16 [384, 12288], P('yz', 'gx')
Inputs may be any that keep to these rules, and one draw needn't show every extreme that they name: `counts`: each group has 1 to 8 valid rows, its first ones; 192 valid rows in all; some group is full.
All inputs are finite; a program needn't handle non-finite values.
Results may differ from a plain program's by a relative error of at most 0.005.
Values may be sent and summed in bfloat16 or wider, within the bound.
No kernel may reach another device: no remote copies, remote signals or barrier semaphores. Data moves between devices by JAX's collectives and lax.ppermute only.
A program may use at most 32 MiB of HBM per device.

v0:
```python
import jax
import jax.numpy as jnp
from jax import lax
from jax.sharding import PartitionSpec as P

GROUP_ROWS = 8


def valid_flags(counts, total_rows):
    row_ids = jnp.arange(total_rows, dtype=jnp.int32)
    groups = row_ids // GROUP_ROWS
    hits = groups[:, None] == jnp.arange(counts.shape[0], dtype=jnp.int32)[None, :]
    row_count = jnp.sum(jnp.where(hits, counts[None, :], 0), axis=1)
    return row_ids - groups * GROUP_ROWS < row_count


def activate(partial_value):
    shares = lax.psum_scatter(partial_value, "gx", scatter_dimension=2, tiled=True)
    hidden_share = (jax.nn.silu(shares[:, 0]) * shares[:, 1]).astype(jnp.bfloat16)
    return lax.all_gather(hidden_share, "gx", axis=1, tiled=True)


def shards(tokens, counts, gate_weight, up_weight, down_weight):
    local_rows = tokens.shape[0]
    total_rows = local_rows * lax.axis_size("yz")
    first_row = lax.axis_index("yz") * local_rows
    valid_all = valid_flags(counts, total_rows)
    own_valid = lax.dynamic_slice_in_dim(valid_all, first_row, local_rows, 0)
    masked = jnp.where(own_valid[:, None], tokens, jnp.zeros_like(tokens))
    piece = lax.all_gather(masked, "yz", axis=0, tiled=True)
    gate_part = jnp.dot(piece, gate_weight, preferred_element_type=jnp.float32)
    up_part = jnp.dot(piece, up_weight, preferred_element_type=jnp.float32)
    partial_value = jnp.stack((gate_part, up_part), axis=1)
    hidden = activate(partial_value)
    return lax.psum_scatter(
        jnp.dot(hidden, down_weight, preferred_element_type=jnp.float32),
        "yz",
        scatter_dimension=0,
        tiled=True,
    ).astype(jnp.bfloat16)


def solution(mesh):
    placed = (P("yz", "gx"), P(), P("gx", "yz"), P("gx", "yz"), P("yz", "gx"))
    return jax.shard_map(
        shards, mesh=mesh, in_specs=placed, out_specs=P("yz", "gx"), check_vma=False
    )
```

profile of v0, /device:TPU:1, one launch (start us, length us, event | category | flops | bytes accessed | tf_op | source)
XLA Modules:
  0.0 1011.7 jit_solution(4277274420895261112)
XLA Ops:
  6.5 0.0 copy-start
  6.5 0.9 select_reduce_fusion
  7.4 0.1 dynamic_slice.3
  7.5 1.4 fusion.1
  8.9 0.0 all-gather.3.cloned.1.call-update
  8.9 0.0 copy-start.2
  8.9 0.0 all-reduce.5.cloned.1.call-start
  9.0 132.2 %all-gather.3.cloned.1.call-done = bf16[192,2,3072]{2,1,0:T(2,128)(2,1)} async-done(((bf16[1,2,3072]{2,1,0:T(2,128)(2,1)}), bf16[192,2,3072]{2,1,0:T(2,128)(2,1)}) %all-gather.3.cloned.1.call-update) | async-done | bytes 2359312 | tf_op jit(solution)/shard_map/all_gather | solution.py:30
  141.2 6.0 reshape.16
  147.2 0.0 copy-done.2
  147.2 2.6 convolution_bitcast_fusion
  149.8 0.2 copy-done.3
  150.1 0.8 convolution_bitcast_fusion.1
  150.8 0.1 pad_maximum_fusion
  150.9 1.2 copy.8
  152.1 0.0 all-reduce.5.cloned.1.call-update
  152.1 1.3 dynamic-slice.2
  153.5 1.3 dynamic-slice
  156.0 51.8 %all-reduce.5.cloned.1.call-done = f32[384,2,256]{0,1,2:T(2,128)} async-done(((f32[384,2,256]{0,1,2:T(2,128)}), f32[384,2,256]{0,1,2:T(2,128)}) %all-reduce.5.cloned.1.call-update) | async-done | bytes 786448
  207.8 1.2 constant_dynamic-slice_fusion
  209.1 9.2 all_gather.7
  218.3 2.9 fusion.6
  221.2 782.2 %all-reduce.6 = bf16[384,3072]{1,0:T(8,128)(2,1)} all-reduce(f32[384,3072]{1,0:T(8,128)} %fusion.6), channel_id=3, replica_groups=mesh['gx'=4,'yz'=192] {'yz'}, use_global_device_ids=true, to_apply=%region_2.3.clone | all-reduce | flops 1179648 | bytes 7077888
  1003.5 1.4 dynamic-slice_convert_fusion
  (8 shorter events, 0.1 us)
Async XLA Ops:
  6.5 211.8 %copy-start = (bf16[256,3072]{1,0:T(8,128)(2,1)S(1)}, bf16[256,3072]{1,0:T(8,128)(2,1)}, u32[]{:S(2)}) copy-start(bf16[256,3072]{1,0:T(8,128)(2,1)} %param.9) | copy-start | bytes 4718596
  6.5 134.7 %all-gather.3.cloned.1.call-start = ((), (), s32[]{:S(2)}) async-start(), calls=%async_computation | async-start | bytes 2371584 | tf_op jit(solution)/shard_map/all_gather | solution.py:30
  8.9 138.3 %copy-start.2 = (bf16[3072,256]{1,0:T(8,128)(2,1)S(1)}, bf16[3072,256]{1,0:T(8,128)(2,1)}, u32[]{:S(2)}) copy-start(bf16[3072,256]{1,0:T(8,128)(2,1)} %param.8) | copy-start | bytes 4718596
  8.9 198.9 %all-reduce.5.cloned.1.call-start = ((), (), s32[]{:S(2)}) async-start(), calls=%async_computation.1 | async-start | bytes 1572864
  147.2 2.6 copy-start.1
  147.2 2.8 copy-start.3
Sparse Core Ops, SparseCore 0:
  11.1 130.0 all-gather.2
  152.2 55.5 all-reduce.4
where the time goes:
time: 1020 us; the launch traced here: 1010 us
  blocking collectives  791 us (78%)
  waiting for transfers between devices  184 us (18%)
  between operations  14.8 us (1%)
  local copies, waits for them, and re-layouts  12.7 us (1%)
    unnamed x1, blocking collectives  782 us
    all_gather x1, waiting for transfers between devices, shards(): piece = lax.all_gather(masked, 'yz', axis=0, tiled=True)  132 us
    unnamed x3, waiting for transfers between devices  51.9 us
  transfers between devices with their start and end apart: 2, of which 2 were waited for; matrix products, arithmetic and copies ran while one was open for 0% of the time, Pallas kernels for 0%

commit v1 on v0

v1 whole, which is shorter than its diff:
```python
import jax
import jax.numpy as jnp
from jax import lax
from jax.sharding import Mesh, PartitionSpec as P

GROUP_ROWS = 8
VALID = 192
Y = 8
C = 2
BF = jnp.bfloat16
F32 = jnp.float32


def exchange(x, axis):
    return lax.all_to_all(x, axis, split_axis=0, concat_axis=0, tiled=False)


def swap(x):
    return lax.ppermute(x, "c", [(0, 1), (1, 0)])


def places(counts, row_ids):
    n = counts.shape[0]
    before = jnp.sum(
        jnp.where(jnp.arange(n)[None, :] < jnp.arange(n)[:, None], counts[None, :], 0), axis=1
    )
    group = row_ids // GROUP_ROWS
    offset = row_ids - group * GROUP_ROWS
    hits = group[:, None] == jnp.arange(n, dtype=jnp.int32)[None, :]
    start = jnp.sum(jnp.where(hits, before[None, :], 0), axis=1)
    count = jnp.sum(jnp.where(hits, counts[None, :], 0), axis=1)
    return jnp.where(offset < count, start + offset, -1)


def shards(tokens, counts, gate_weight, up_weight, down_weight):
    rows, width = tokens.shape
    hidden_units = gate_weight.shape[1]
    gx, nz = lax.axis_size("gx"), lax.axis_size("z")
    total = nz * Y * C * rows
    core = lax.axis_index("c")

    by_z = exchange(jnp.broadcast_to(tokens[None], (nz, rows, width)), "z")
    by_z = by_z.reshape(nz * rows, width)
    own = exchange(jnp.broadcast_to(by_z[None], (Y, nz * rows, width)), "y")
    own = own.reshape(Y * nz * rows, width)
    other = swap(own)

    q = jnp.arange(Y * nz * rows, dtype=jnp.int32)
    base = (q // rows % nz) * (Y * C * rows) + (q // (rows * nz)) * (C * rows) + q % rows
    slots = jnp.arange(VALID, dtype=jnp.int32)[:, None]
    pick_own = (slots == places(counts, base + core * rows)[None, :]).astype(BF)
    pick_other = (slots == places(counts, base + (1 - core) * rows)[None, :]).astype(BF)
    x = (
        jnp.dot(pick_own, own, preferred_element_type=F32)
        + jnp.dot(pick_other, other, preferred_element_type=F32)
    ).astype(BF)

    part = hidden_units // gx
    gate = jnp.dot(x, gate_weight, preferred_element_type=F32).reshape(VALID, gx, part)
    up = jnp.dot(x, up_weight, preferred_element_type=F32).reshape(VALID, gx, part)
    both = jnp.concatenate((gate, up), axis=2).transpose(1, 0, 2)
    sums = jnp.sum(exchange(both, "gx"), axis=0)
    share = (jax.nn.silu(sums[:, :part]) * sums[:, part:]).astype(BF)
    hidden = lax.all_gather(share, "gx", axis=1, tiled=True)

    half = width // C
    w_own = lax.dynamic_slice_in_dim(down_weight, core * half, half, 1)
    w_other = lax.dynamic_slice_in_dim(down_weight, (1 - core) * half, half, 1)
    away = jnp.dot(hidden, w_other, preferred_element_type=F32).astype(BF)
    here = jnp.dot(hidden, w_own, preferred_element_type=F32)
    pair = here + swap(away).astype(F32)
    block = half // Y
    pieces = pair.astype(BF).reshape(VALID, Y, block).transpose(1, 0, 2)
    column = jnp.sum(exchange(pieces, "y").astype(F32), axis=0).astype(BF)

    everywhere = places(counts, jnp.arange(total, dtype=jnp.int32))
    spread = (everywhere[:, None] == jnp.arange(VALID, dtype=jnp.int32)[None, :]).astype(BF)
    padded = jnp.dot(spread, column, preferred_element_type=F32).astype(BF)
    padded = padded.reshape(nz, Y * C * rows, block)
    summed = jnp.sum(exchange(padded, "z").astype(F32), axis=0).astype(BF)
    mine = exchange(summed.reshape(Y * C, rows, block), ("y", "c"))
    mine = mine.reshape(Y, C, rows, block).transpose(2, 1, 0, 3)
    return mine.reshape(rows, width)


def solution(mesh):
    gx, yz = mesh.shape["gx"], mesh.shape["yz"]
    fine = Mesh(mesh.devices.reshape(gx, yz // (Y * C), Y, C), ("gx", "z", "y", "c"))
    line = ("z", "y", "c")
    placed = (P(line, "gx"), P(), P("gx", line), P("gx", line), P(line, "gx"))
    return jax.shard_map(
        shards, mesh=fine, in_specs=placed, out_specs=P(line, "gx"), check_vma=False
    )
```

time: 1020 us -> 165 us (0.16)
  blocking collectives: 791 us -> 99.2 us
  waiting for transfers between devices: 184 us -> 34 us
  starting transfers between devices: 0.04 us -> 20.2 us
  between operations: 14.8 us -> 0.23 us
    unnamed x1 -> x0, blocking collectives: 782 us -> none
    all_gather x1 -> x0, waiting for transfers between devices: 132 us -> none  [shards(): piece = lax.all_gather(masked, 'yz', axis=0, tiled=True)]
    all_to_all x0 -> x4, blocking collectives: none -> 90 us  [exchange(): return lax.all_to_all(x, axis, split_axis=0, concat_axis=0, tiled=False)]
    unnamed x3 -> x0, waiting for transfers between devices: 51.9 us -> none
    all_to_all x0 -> x2, waiting for transfers between devices: none -> 30.6 us  [exchange(): return lax.all_to_all(x, axis, split_axis=0, concat_axis=0, tiled=False)]
    ppermute x0 -> x2, starting transfers between devices: none -> 12.7 us  [swap(): return lax.ppermute(x, 'c', [(0, 1), (1, 0)])]
  transfers between devices with their start and end apart: 2 -> 4, of which waited for: 2 -> 4; matrix products, arithmetic and copies ran while one was open for 0% -> 1% of each run, Pallas kernels for 0% -> 0%
where the time goes in v1:
time: 165 us
  blocking collectives  99.2 us (60%)
  waiting for transfers between devices  34 us (21%)
  starting transfers between devices  20.2 us (12%)
  local copies, waits for them, and re-layouts  5.43 us (3%)
  matrix products  4.85 us (3%)
    all_to_all x4, blocking collectives, exchange(): return lax.all_to_all(x, axis, split_axis=0, concat_axis=0, tiled=False)  90 us
    all_to_all x2, waiting for transfers between devices, exchange(): return lax.all_to_all(x, axis, split_axis=0, concat_axis=0, tiled=False)  30.6 us
    ppermute x2, starting transfers between devices, swap(): return lax.ppermute(x, 'c', [(0, 1), (1, 0)])  12.7 us
    all_gather x1, blocking collectives, shards(): hidden = lax.all_gather(share, 'gx', axis=1, tiled=True)  9.11 us
    all_to_all x2, starting transfers between devices, exchange(): return lax.all_to_all(x, axis, split_axis=0, concat_axis=0, tiled=False)  7.56 us
    ppermute x2, waiting for transfers between devices, swap(): return lax.ppermute(x, 'c', [(0, 1), (1, 0)])  3.4 us
  transfers between devices with their start and end apart: 4, of which 4 were waited for; matrix products, arithmetic and copies ran while one was open for 1% of the time, Pallas kernels for 0%

profile of v1, /device:TPU:1, one launch (start us, length us, event | category | flops | bytes accessed | tf_op | source)
XLA Modules:
  0.0 164.6 jit_solution(15348390695715343355)
XLA Ops:
  0.0 0.9 broadcast_in_dim.116
  0.9 26.9 %all_to_all.30 = bf16[12,2,3072]{2,1,0:T(2,128)(2,1)S(1)} all-to-all(bf16[12,2,3072]{2,1,0:T(2,128)(2,1)S(1)} %broadcast_in_dim.116), channel_id=1, replica_groups=mesh['gx'=4,'z'=12,'y'=8,'c'=2] {'z'}, dimensions={0} | all-to-all | bytes 294912 | tf_op jit(solution)/shard_map/all_to_all | solution.py:15
  28.0 35.0 %all_to_all.31 = bf16[8,24,3072]{2,1,0:T(8,128)(2,1)S(1)} all-to-all(bf16[8,24,3072]{2,1,0:T(8,128)(2,1)S(1)} %broadcast_in_dim.118), channel_id=1, replica_groups=mesh['gx'=4,'z'=12,'y'=8,'c'=2] {'y'}, dimensions={0} | all-to-all | bytes 2359296 | tf_op jit(solution)/shard_map/all_to_all | solution.py:15
  62.9 6.1 %collective-permute-start = (bf16[192,3072]{1,0:T(8,128)(2,1)S(1)}, bf16[192,3072]{1,0:T(8,128)(2,1)}, u32[]{:S(2)}, u32[]{:S(2)}) collective-permute-start(bf16[192,3072]{1,0:T(8,128)(2,1)S(1)} %bitcast.23), channel_id=1, source_target_pairs={{0,1},{1,0},{2,3},{3,2},{4,5},{5,4},{6,7},{7,6},{8,9},{9,8},{10,11... | collective-permute-start | bytes 3538952 | tf_op jit(solution)/shard_map/ppermute | solution.py:19
  69.3 0.5 fusion.7
  69.8 1.8 %collective-permute-done = bf16[192,3072]{1,0:T(8,128)(2,1)} collective-permute-done((bf16[192,3072]{1,0:T(8,128)(2,1)S(1)}, bf16[192,3072]{1,0:T(8,128)(2,1)}, u32[]{:S(2)}, u32[]{:S(2)}) %collective-permute-start) | collective-permute-done | bytes 1179680 | tf_op jit(solution)/shard_map/ppermute | solution.py:19
  71.6 1.9 %fusion = bf16[192,3072]{1,0:T(8,128)(2,1)S(1)} fusion(f32[192,3072]{1,0:T(8,128)S(1)} %fusion.7, bf16[192,3072]{1,0:T(8,128)(2,1)} %collective-permute-done, s32[192]{0:T(256)S(1)} %get-tuple-element.15), kind=kOutput, calls=%fused_computation.1 | convolution fusion | flops 227708928 | bytes 4719360 | tf_op jit(solution)/shard_map/dot_general | solution.py:55
  73.5 0.7 fusion.25
  74.2 0.7 copy-done.2
  74.9 0.7 fusion.24
  75.7 0.9 copy.22
  76.6 4.0 %all-to-all-start.2 = ((f32[4,192,128]{2,1,0:T(8,128)}), f32[4,192,128]{2,1,0:T(8,128)S(1)}, u32[]{:S(2)}, u32[]{:S(2)}) async-start(f32[4,192,128]{2,1,0:T(8,128)} %copy.22), calls=%async_computation.2 | async-start | bytes 786432 | tf_op jit(solution)/shard_map/all_to_all | solution.py:15
  80.6 7.2 %all-to-all-done.2 = f32[4,192,128]{2,1,0:T(8,128)S(1)} async-done(((f32[4,192,128]{2,1,0:T(8,128)}), f32[4,192,128]{2,1,0:T(8,128)S(1)}, u32[]{:S(2)}, u32[]{:S(2)}) %all-to-all-start.2) | async-done | bytes 393248 | tf_op jit(solution)/shard_map/all_to_all | solution.py:15
  88.2 9.1 %all_gather.3 = bf16[192,256]{0,1:T(8,128)(2,1)S(1)} all-gather(bf16[192,64]{0,1:T(8,128)(2,1)S(1)} %multiply_convert_fusion), channel_id=1, replica_groups=mesh['gx'=4,'z'=12,'y'=8,'c'=2] {'gx'}, dimensions={1}, use_global_device_ids=true | all-gather | bytes 122880 | tf_op jit(solution)/shard_map/all_gather | solution.py:64
  97.6 6.6 %collective-permute-start.1 = (bf16[192,1536]{1,0:T(8,128)(2,1)S(1)}, bf16[192,1536]{1,0:T(8,128)(2,1)S(1)}, u32[]{:S(2)}, u32[]{:S(2)}) collective-permute-start(bf16[192,1536]{1,0:T(8,128)(2,1)S(1)} %convolution_convert_fusion), channel_id=1, source_target_pairs={{0,1},{1,0},{2,3},{3,2},{4,5},{5,4},{6,7},{7,6},{8,9},{9,8},{10,11... | collective-permute-start | bytes 1769480 | tf_op jit(solution)/shard_map/ppermute | solution.py:19
  104.3 1.6 collective-permute-done.1
  105.9 0.3 add_convert_fusion
  106.2 0.6 reshape.218
  106.8 1.0 copy.33
  107.9 3.5 %all-to-all-start.3 = ((bf16[8,192,192]{2,1,0:T(8,128)(2,1)}), bf16[8,192,192]{2,1,0:T(8,128)(2,1)S(1)}, u32[]{:S(2)}, u32[]{:S(2)}) async-start(bf16[8,192,192]{2,1,0:T(8,128)(2,1)} %bitcast.22), calls=%async_computation.3 | async-start | bytes 1572864 | tf_op jit(solution)/shard_map/all_to_all | solution.py:15
  111.5 23.4 %all-to-all-done.3 = bf16[8,192,192]{2,1,0:T(8,128)(2,1)S(1)} async-done(((bf16[8,192,192]{2,1,0:T(8,128)(2,1)}), bf16[8,192,192]{2,1,0:T(8,128)(2,1)S(1)}, u32[]{:S(2)}, u32[]{:S(2)}) %all-to-all-start.3) | async-done | bytes 589856 | tf_op jit(solution)/shard_map/all_to_all | solution.py:15
  135.6 16.1 %all_to_all.32 = bf16[12,32,192]{2,1,0:T(8,128)(2,1)S(1)} all-to-all(bf16[12,32,192]{2,1,0:T(8,128)(2,1)S(1)} %bitcast.27), channel_id=1, replica_groups=mesh['gx'=4,'z'=12,'y'=8,'c'=2] {'z'}, dimensions={0} | all-to-all | bytes 294912 | tf_op jit(solution)/shard_map/all_to_all | solution.py:15
  151.7 12.2 %all_to_all.33 = bf16[16,2,192]{2,1,0:T(2,128)(2,1)S(1)} all-to-all(bf16[16,2,192]{2,1,0:T(2,128)(2,1)S(1)} %reshape.220), channel_id=1, replica_groups=mesh['gx'=4,'z'=12,'y'=8,'c'=2] {'y','c'}, dimensions={0} | all-to-all | bytes 24576 | tf_op jit(solution)/shard_map/all_to_all | solution.py:15
  163.9 0.7 reshape.222
  (30 shorter events, 1.9 us)
Async XLA Ops:
  0.0 97.3 %copy-start = (bf16[256,3072]{1,0:T(8,128)(2,1)S(1)}, bf16[256,3072]{1,0:T(8,128)(2,1)}, u32[]{:S(2)}) copy-start(bf16[256,3072]{1,0:T(8,128)(2,1)} %param.9) | copy-start | bytes 4718596
  28.0 41.1 %copy-start.3 = (s32[48]{0:T(128)S(1)}, s32[48]{0:T(128)}, u32[]{:S(2)}) copy-start(s32[48]{0:T(128)} %param.6) | copy-start | bytes 580
  62.9 8.6 %collective-permute-start = (bf16[192,3072]{1,0:T(8,128)(2,1)S(1)}, bf16[192,3072]{1,0:T(8,128)(2,1)}, u32[]{:S(2)}, u32[]{:S(2)}) collective-permute-start(bf16[192,3072]{1,0:T(8,128)(2,1)S(1)} %bitcast.23), channel_id=1, source_target_pairs={{0,1},{1,0},{2,3},{3,2},{4,5},{5,4},{6,7},{7,6},{8,9},{9,8},{10,11... | collective-permute-start | bytes 3538952 | tf_op jit(solution)/shard_map/ppermute | solution.py:19
  71.6 1.9 %copy-start.1 = (bf16[3072,256]{1,0:T(8,128)(2,1)S(1)}, bf16[3072,256]{1,0:T(8,128)(2,1)}, u32[]{:S(2)}) copy-start(bf16[3072,256]{1,0:T(8,128)(2,1)} %param.8) | copy-start | bytes 4718596
  73.5 1.4 copy-start.2
  76.6 11.2 %all-to-all-start.2 = ((f32[4,192,128]{2,1,0:T(8,128)}), f32[4,192,128]{2,1,0:T(8,128)S(1)}, u32[]{:S(2)}, u32[]{:S(2)}) async-start(f32[4,192,128]{2,1,0:T(8,128)} %copy.22), calls=%async_computation.2 | async-start | bytes 786432 | tf_op jit(solution)/shard_map/all_to_all | solution.py:15
  97.6 8.2 %collective-permute-start.1 = (bf16[192,1536]{1,0:T(8,128)(2,1)S(1)}, bf16[192,1536]{1,0:T(8,128)(2,1)S(1)}, u32[]{:S(2)}, u32[]{:S(2)}) collective-permute-start(bf16[192,1536]{1,0:T(8,128)(2,1)S(1)} %convolution_convert_fusion), channel_id=1, source_target_pairs={{0,1},{1,0},{2,3},{3,2},{4,5},{5,4},{6,7},{7,6},{8,9},{9,8},{10,11... | collective-permute-start | bytes 1769480 | tf_op jit(solution)/shard_map/ppermute | solution.py:19
  107.9 27.1 %all-to-all-start.3 = ((bf16[8,192,192]{2,1,0:T(8,128)(2,1)}), bf16[8,192,192]{2,1,0:T(8,128)(2,1)S(1)}, u32[]{:S(2)}, u32[]{:S(2)}) async-start(bf16[8,192,192]{2,1,0:T(8,128)(2,1)} %bitcast.22), calls=%async_computation.3 | async-start | bytes 1572864 | tf_op jit(solution)/shard_map/all_to_all | solution.py:15

commit v2 on v1

--- a/solution.py
+++ b/solution.py
@@ -9,6 +9,7 @@
 C = 2
 BF = jnp.bfloat16
 F32 = jnp.float32
+SCALE = 32.0
 
 
 def exchange(x, axis):
@@ -55,32 +56,45 @@
         + jnp.dot(pick_other, other, preferred_element_type=F32)
     ).astype(BF)
 
-    part = hidden_units // gx
-    gate = jnp.dot(x, gate_weight, preferred_element_type=F32).reshape(VALID, gx, part)
-    up = jnp.dot(x, up_weight, preferred_element_type=F32).reshape(VALID, gx, part)
-    both = jnp.concatenate((gate, up), axis=2).transpose(1, 0, 2)
-    sums = jnp.sum(exchange(both, "gx"), axis=0)
-    share = (jax.nn.silu(sums[:, :part]) * sums[:, part:]).astype(BF)
-    hidden = lax.all_gather(share, "gx", axis=1, tiled=True)
+    gate = jnp.dot(x, gate_weight, preferred_element_type=F32)
+    up = jnp.dot(x, up_weight, preferred_element_type=F32)
+    partial = (jnp.concatenate((gate, up), axis=1) * SCALE).astype(jnp.float16)
+    parts = lax.all_gather(partial, "gx", axis=0, tiled=False)
+    sums = jnp.sum(parts.astype(F32), axis=0) * (1.0 / SCALE)
+    hidden = (jax.nn.silu(sums[:, :hidden_units]) * sums[:, hidden_units:]).astype(BF)
 
     half = width // C
     w_own = lax.dynamic_slice_in_dim(down_weight, core * half, half, 1)
     w_other = lax.dynamic_slice_in_dim(down_weight, (1 - core) * half, half, 1)
     away = jnp.dot(hidden, w_other, preferred_element_type=F32).astype(BF)
     here = jnp.dot(hidden, w_own, preferred_element_type=F32)
-    pair = here + swap(away).astype(F32)
-    block = half // Y
-    pieces = pair.astype(BF).reshape(VALID, Y, block).transpose(1, 0, 2)
+    pair = (here + swap(away).astype(F32)).astype(BF)
+
+    tile = half // Y * 2 // 3
+    tiles = pair.reshape(VALID, half // tile, tile).transpose(1, 0, 2)
+    seconds = tiles[Y:].reshape(Y, VALID // 2, tile)
+    pieces = jnp.concatenate((tiles[:Y], seconds), axis=1)
     column = jnp.sum(exchange(pieces, "y").astype(F32), axis=0).astype(BF)
 
     everywhere = places(counts, jnp.arange(total, dtype=jnp.int32))
-    spread = (everywhere[:, None] == jnp.arange(VALID, dtype=jnp.int32)[None, :]).astype(BF)
-    padded = jnp.dot(spread, column, preferred_element_type=F32).astype(BF)
-    padded = padded.reshape(nz, Y * C * rows, block)
+    slots = jnp.arange(VALID, dtype=jnp.int32)
+    spread = (everywhere[:, None] == slots[None, :]).astype(BF)
+    first_slot = lax.axis_index("y") % 2 * (VALID // 2)
+    spread_half = (everywhere[:, None] == first_slot + slots[None, : VALID // 2]).astype(BF)
+    padded = jnp.concatenate(
+        (
+            jnp.dot(spread, column[:VALID], preferred_element_type=F32).astype(BF),
+            jnp.dot(spread_half, column[VALID:], preferred_element_type=F32).astype(BF),
+        ),
+        axis=1,
+    ).reshape(nz, Y * C * rows, 2 * tile)
     summed = jnp.sum(exchange(padded, "z").astype(F32), axis=0).astype(BF)
-    mine = exchange(summed.reshape(Y * C, rows, block), ("y", "c"))
-    mine = mine.reshape(Y, C, rows, block).transpose(2, 1, 0, 3)
-    return mine.reshape(rows, width)
+    mine = exchange(summed.reshape(Y * C, rows, 2 * tile), ("y", "c"))
+    mine = mine.reshape(Y, C, rows, 2, tile)
+    firsts = mine[:, :, :, 0].transpose(2, 1, 0, 3)
+    pairs = mine[:, :, :, 1].reshape(Y // 2, 2, C, rows, tile)
+    seconds = (pairs[:, 0] + pairs[:, 1]).transpose(2, 1, 0, 3)
+    return jnp.concatenate((firsts, seconds), axis=2).reshape(rows, width)
 
 
 def solution(mesh):

time: 165 us -> 149 us (0.903)
  waiting for transfers between devices: 34 us -> 22.6 us
  starting transfers between devices: 20.2 us -> 13.8 us
  blocking collectives: 99.2 us -> 102 us
    all_to_all x2 -> x1, waiting for transfers between devices: 30.6 us -> 19.2 us  [exchange(): return lax.all_to_all(x, axis, split_axis=0, concat_axis=0, tiled=False)]
    all_to_all x2 -> x1, starting transfers between devices: 7.56 us -> 3.54 us  [exchange(): return lax.all_to_all(x, axis, split_axis=0, concat_axis=0, tiled=False)]
    all_gather x1, blocking collectives: 9.11 us -> 12 us  [shards(): parts = lax.all_gather(partial, 'gx', axis=0, tiled=False)]
    ppermute x2, starting transfers between devices: 12.7 us -> 10.2 us  [swap(): return lax.ppermute(x, 'c', [(0, 1), (1, 0)])]
  transfers between devices with their start and end apart: 4 -> 3, of which waited for: 4 -> 3; matrix products, arithmetic and copies ran while one was open for 1% -> 1% of each run, Pallas kernels for 0% -> 0%
where the time goes in v2:
time: 149 us; the launch traced here: 148 us
  blocking collectives  102 us (68%)
  waiting for transfers between devices  22.6 us (15%)
  starting transfers between devices  13.8 us (9%)
  matrix products  4.56 us (3%)
  local copies, waits for them, and re-layouts  4.36 us (3%)
    all_to_all x4, blocking collectives, exchange(): return lax.all_to_all(x, axis, split_axis=0, concat_axis=0, tiled=False)  90 us
    all_to_all x1, waiting for transfers between devices, exchange(): return lax.all_to_all(x, axis, split_axis=0, concat_axis=0, tiled=False)  19.2 us
    all_gather x1, blocking collectives, shards(): parts = lax.all_gather(partial, 'gx', axis=0, tiled=False)  12 us
    ppermute x2, starting transfers between devices, swap(): return lax.ppermute(x, 'c', [(0, 1), (1, 0)])  10.2 us
    all_to_all x1, starting transfers between devices, exchange(): return lax.all_to_all(x, axis, split_axis=0, concat_axis=0, tiled=False)  3.54 us
    ppermute x2, waiting for transfers between devices, swap(): return lax.ppermute(x, 'c', [(0, 1), (1, 0)])  3.39 us
  transfers between devices with their start and end apart: 3, of which 3 were waited for; matrix products, arithmetic and copies ran while one was open for 1% of the time, Pallas kernels for 0%

profile of v2, /device:TPU:1, one launch (start us, length us, event | category | flops | bytes accessed | tf_op | source)
XLA Modules:
  0.0 148.5 jit_solution(7970967500973755465)
XLA Ops:
  0.0 0.9 broadcast_in_dim.118
  0.9 26.9 %all_to_all.25 = bf16[12,2,3072]{2,1,0:T(2,128)(2,1)S(1)} all-to-all(bf16[12,2,3072]{2,1,0:T(2,128)(2,1)S(1)} %broadcast_in_dim.118), channel_id=1, replica_groups=mesh['gx'=4,'z'=12,'y'=8,'c'=2] {'z'}, dimensions={0} | all-to-all | bytes 294912 | tf_op jit(solution)/shard_map/all_to_all | solution.py:16
  28.0 35.0 %all_to_all.26 = bf16[8,24,3072]{2,1,0:T(8,128)(2,1)S(1)} all-to-all(bf16[8,24,3072]{2,1,0:T(8,128)(2,1)S(1)} %broadcast_in_dim.120), channel_id=1, replica_groups=mesh['gx'=4,'z'=12,'y'=8,'c'=2] {'y'}, dimensions={0} | all-to-all | bytes 2359296 | tf_op jit(solution)/shard_map/all_to_all | solution.py:16
  62.9 6.1 %collective-permute-start = (bf16[192,3072]{1,0:T(8,128)(2,1)S(1)}, bf16[192,3072]{1,0:T(8,128)(2,1)}, u32[]{:S(2)}, u32[]{:S(2)}) collective-permute-start(bf16[192,3072]{1,0:T(8,128)(2,1)S(1)} %bitcast.26), channel_id=1, source_target_pairs={{0,1},{1,0},{2,3},{3,2},{4,5},{5,4},{6,7},{7,6},{8,9},{9,8},{10,11... | collective-permute-start | bytes 3538952 | tf_op jit(solution)/shard_map/ppermute | solution.py:20
  69.3 0.5 fusion.9
  69.8 1.8 %collective-permute-done = bf16[192,3072]{1,0:T(8,128)(2,1)} collective-permute-done((bf16[192,3072]{1,0:T(8,128)(2,1)S(1)}, bf16[192,3072]{1,0:T(8,128)(2,1)}, u32[]{:S(2)}, u32[]{:S(2)}) %collective-permute-start) | collective-permute-done | bytes 1179680 | tf_op jit(solution)/shard_map/ppermute | solution.py:20
  71.6 1.9 %fusion = bf16[192,3072]{1,0:T(8,128)(2,1)S(1)} fusion(f32[192,3072]{1,0:T(8,128)S(1)} %fusion.9, bf16[192,3072]{1,0:T(8,128)(2,1)} %collective-permute-done, s32[192]{0:T(256)S(1)} %get-tuple-element.17), kind=kOutput, calls=%fused_computation.1 | convolution fusion | flops 227708928 | bytes 4719360 | tf_op jit(solution)/shard_map/dot_general | solution.py:56
  73.5 0.5 convolution_bitcast_fusion
  74.0 0.9 copy-done.2
  74.9 0.5 convolution_bitcast_fusion.1
  75.4 12.0 %all_gather.4 = f16[4,192,512]{2,1,0:T(8,128)(2,1)S(1)} all-gather(f16[1,192,512]{2,1,0:T(8,128)(2,1)S(1)} %fusion.6), channel_id=1, replica_groups=mesh['gx'=4,'z'=12,'y'=8,'c'=2] {'gx'}, dimensions={0}, use_global_device_ids=true | all-gather | bytes 983040 | tf_op jit(solution)/shard_map/all_gather | solution.py:62
  87.6 0.3 convolution_convert_fusion
  88.0 4.2 %collective-permute-start.1 = (bf16[192,1536]{1,0:T(8,128)(2,1)S(1)}, bf16[192,1536]{1,0:T(8,128)(2,1)S(1)}, u32[]{:S(2)}, u32[]{:S(2)}) collective-permute-start(bf16[192,1536]{1,0:T(8,128)(2,1)S(1)} %convolution_convert_fusion), channel_id=1, source_target_pairs={{0,1},{1,0},{2,3},{3,2},{4,5},{5,4},{6,7},{7,6},{8,9},{9,8},{10,11... | collective-permute-start | bytes 1769480 | tf_op jit(solution)/shard_map/ppermute | solution.py:20
  92.2 1.6 %collective-permute-done.1 = bf16[192,1536]{1,0:T(8,128)(2,1)S(1)} collective-permute-done((bf16[192,1536]{1,0:T(8,128)(2,1)S(1)}, bf16[192,1536]{1,0:T(8,128)(2,1)S(1)}, u32[]{:S(2)}, u32[]{:S(2)}) %collective-permute-start.1) | collective-permute-done | bytes 589856 | tf_op jit(solution)/shard_map/ppermute | solution.py:20
  93.8 0.3 add_convert_fusion
  94.1 0.4 reshape.248
  94.8 0.9 copy.34
  95.7 3.5 %all-to-all-start.2 = ((bf16[8,288,128]{2,1,0:T(8,128)(2,1)}), bf16[8,288,128]{2,1,0:T(8,128)(2,1)S(1)}, u32[]{:S(2)}, u32[]{:S(2)}) async-start(bf16[8,288,128]{2,1,0:T(8,128)(2,1)} %copy.34), calls=%async_computation.2 | async-start | bytes 1179648 | tf_op jit(solution)/shard_map/all_to_all | solution.py:16
  99.4 19.2 %all-to-all-done.2 = bf16[8,288,128]{2,1,0:T(8,128)(2,1)S(1)} async-done(((bf16[8,288,128]{2,1,0:T(8,128)(2,1)}), bf16[8,288,128]{2,1,0:T(8,128)(2,1)S(1)}, u32[]{:S(2)}, u32[]{:S(2)}) %all-to-all-start.2) | async-done | bytes 589856 | tf_op jit(solution)/shard_map/all_to_all | solution.py:16
  118.7 0.3 convolution_convert_fusion.2
  119.0 0.3 convolution_convert_fusion.1
  119.5 16.1 %all_to_all.27 = bf16[12,32,256]{2,1,0:T(8,128)(2,1)S(1)} all-to-all(bf16[12,32,256]{2,1,0:T(8,128)(2,1)S(1)} %bitcast.31), channel_id=1, replica_groups=mesh['gx'=4,'z'=12,'y'=8,'c'=2] {'z'}, dimensions={0} | all-to-all | bytes 393216 | tf_op jit(solution)/shard_map/all_to_all | solution.py:16
  135.6 12.2 %all_to_all.28 = bf16[16,2,256]{2,1,0:T(2,128)(2,1)S(1)} all-to-all(bf16[16,2,256]{2,1,0:T(2,128)(2,1)S(1)} %reshape.251), channel_id=1, replica_groups=mesh['gx'=4,'z'=12,'y'=8,'c'=2] {'y','c'}, dimensions={0} | all-to-all | bytes 32768 | tf_op jit(solution)/shard_map/all_to_all | solution.py:16
  147.9 0.6 reshape.253
  (41 shorter events, 1.5 us)
Async XLA Ops:
  0.0 87.6 %copy-start = (bf16[256,3072]{1,0:T(8,128)(2,1)S(1)}, bf16[256,3072]{1,0:T(8,128)(2,1)}, u32[]{:S(2)}) copy-start(bf16[256,3072]{1,0:T(8,128)(2,1)} %param.9) | copy-start | bytes 4718596
  28.0 41.1 %copy-start.3 = (s32[48]{0:T(128)S(1)}, s32[48]{0:T(128)}, u32[]{:S(2)}) copy-start(s32[48]{0:T(128)} %param.6) | copy-start | bytes 580
  62.9 8.6 %collective-permute-start = (bf16[192,3072]{1,0:T(8,128)(2,1)S(1)}, bf16[192,3072]{1,0:T(8,128)(2,1)}, u32[]{:S(2)}, u32[]{:S(2)}) collective-permute-start(bf16[192,3072]{1,0:T(8,128)(2,1)S(1)} %bitcast.26), channel_id=1, source_target_pairs={{0,1},{1,0},{2,3},{3,2},{4,5},{5,4},{6,7},{7,6},{8,9},{9,8},{10,11... | collective-permute-start | bytes 3538952 | tf_op jit(solution)/shard_map/ppermute | solution.py:20
  71.6 1.9 %copy-start.1 = (bf16[3072,256]{1,0:T(8,128)(2,1)S(1)}, bf16[3072,256]{1,0:T(8,128)(2,1)}, u32[]{:S(2)}) copy-start(bf16[3072,256]{1,0:T(8,128)(2,1)} %param.8) | copy-start | bytes 4718596
  73.5 1.4 copy-start.2
  88.0 5.8 %collective-permute-start.1 = (bf16[192,1536]{1,0:T(8,128)(2,1)S(1)}, bf16[192,1536]{1,0:T(8,128)(2,1)S(1)}, u32[]{:S(2)}, u32[]{:S(2)}) collective-permute-start(bf16[192,1536]{1,0:T(8,128)(2,1)S(1)} %convolution_convert_fusion), channel_id=1, source_target_pairs={{0,1},{1,0},{2,3},{3,2},{4,5},{5,4},{6,7},{7,6},{8,9},{9,8},{10,11... | collective-permute-start | bytes 1769480 | tf_op jit(solution)/shard_map/ppermute | solution.py:20
  95.7 22.9 %all-to-all-start.2 = ((bf16[8,288,128]{2,1,0:T(8,128)(2,1)}), bf16[8,288,128]{2,1,0:T(8,128)(2,1)S(1)}, u32[]{:S(2)}, u32[]{:S(2)}) async-start(bf16[8,288,128]{2,1,0:T(8,128)(2,1)} %copy.34), calls=%async_computation.2 | async-start | bytes 1179648 | tf_op jit(solution)/shard_map/all_to_all | solution.py:16

commit v3 on v2

v3 whole, which is shorter than its diff:
```python
import jax
import jax.numpy as jnp
from jax import lax
from jax.experimental import pallas as pl
from jax.experimental.pallas import tpu as pltpu
from jax.sharding import Mesh, PartitionSpec as P

GROUP_ROWS = 8
VALID = 192
Y = 8
C = 2
BF = jnp.bfloat16
F32 = jnp.float32
SCALE = 32.0
OVER_ROWS = (((0,), (0,)), ((), ()))


def exchange(x, axis):
    return lax.all_to_all(x, axis, split_axis=0, concat_axis=0, tiled=False)


def swap(x):
    return lax.ppermute(x, "c", [(0, 1), (1, 0)])


def places(counts, row_ids):
    n = counts.shape[0]
    before = jnp.sum(
        jnp.where(jnp.arange(n)[None, :] < jnp.arange(n)[:, None], counts[None, :], 0), axis=1
    )
    group = row_ids // GROUP_ROWS
    offset = row_ids - group * GROUP_ROWS
    hits = group[:, None] == jnp.arange(n, dtype=jnp.int32)[None, :]
    start = jnp.sum(jnp.where(hits, before[None, :], 0), axis=1)
    count = jnp.sum(jnp.where(hits, counts[None, :], 0), axis=1)
    return jnp.where(offset < count, start + offset, -1)


def gate_up(parity, blocks, gate_weight, up_weight):
    count, slots, block = blocks.shape
    units = gate_weight.shape[1]
    step = count // 2
    weight_shape = (count, C, block, units)

    def kernel(parity_ref, x_ref, gate_ref, up_ref, out_ref):
        gate = jnp.zeros((slots, units), F32)
        up = jnp.zeros((slots, units), F32)
        for i in range(step):
            gate += jnp.dot(x_ref[i], gate_ref[i, 0], preferred_element_type=F32)
            up += jnp.dot(x_ref[i], up_ref[i, 0], preferred_element_type=F32)

        @pl.when(pl.program_id(0) == 0)
        def _():
            out_ref[:, :units] = gate
            out_ref[:, units:] = up

        @pl.when(pl.program_id(0) > 0)
        def _():
            out_ref[:, :units] += gate
            out_ref[:, units:] += up

    weights = pl.BlockSpec((step, 1, block, units), lambda i, parity: (i, parity[0], 0, 0))
    return pl.pallas_call(
        kernel,
        out_shape=jax.ShapeDtypeStruct((slots, 2 * units), F32),
        grid_spec=pltpu.PrefetchScalarGridSpec(
            num_scalar_prefetch=1,
            grid=(count // step,),
            in_specs=[pl.BlockSpec((step, slots, block), lambda i, parity: (i, 0, 0)), weights, weights],
            out_specs=pl.BlockSpec((slots, 2 * units), lambda i, parity: (0, 0)),
        ),
        compiler_params=pltpu.CompilerParams(vmem_limit_bytes=32 << 20),
        cost_estimate=pl.CostEstimate(
            flops=4 * slots * count * block * units,
            bytes_accessed=4 * count * block * units,
            transcendentals=0,
        ),
    )(parity[None], blocks, gate_weight.reshape(weight_shape), up_weight.reshape(weight_shape))


def down(core, hidden, down_weight, got, tile):
    slots, units = hidden.shape
    half = got.shape[1]

    def kernel(core_ref, hidden_ref, weight_ref, got_ref, out_ref):
        pair = jnp.dot(hidden_ref[...], weight_ref[...], preferred_element_type=F32)
        pair = (pair + got_ref[...].astype(F32)).astype(BF)
        for i in range(half // tile):
            columns = pair[:, i * tile : (i + 1) * tile]
            if i < Y:
                out_ref[i, :slots] = columns
            else:
                j = 2 * (i - Y)
                out_ref[j, slots:] = columns[: slots // 2]
                out_ref[j + 1, slots:] = columns[slots // 2 :]

    return pl.pallas_call(
        kernel,
        out_shape=jax.ShapeDtypeStruct((Y, slots + slots // 2, tile), BF),
        grid_spec=pltpu.PrefetchScalarGridSpec(
            num_scalar_prefetch=1,
            grid=(1,),
            in_specs=[
                pl.BlockSpec((slots, units), lambda i, core: (0, 0)),
                pl.BlockSpec((units, half), lambda i, core: (0, core[0])),
                pl.BlockSpec((slots, half), lambda i, core: (0, 0)),
            ],
            out_specs=pl.BlockSpec((Y, slots + slots // 2, tile), lambda i, core: (0, 0, 0)),
        ),
        compiler_params=pltpu.CompilerParams(vmem_limit_bytes=32 << 20),
    )(core[None], hidden, down_weight, got)


def shards(tokens, counts, gate_weight, up_weight, down_weight):
    rows, width = tokens.shape
    hidden_units = gate_weight.shape[1]
    gx, nz = lax.axis_size("gx"), lax.axis_size("z")
    total = nz * Y * C * rows
    core = lax.axis_index("c")

    block = width // (Y * C)
    cut = tokens.reshape(rows, Y * C, block).transpose(1, 0, 2)
    near = exchange(cut, ("y", "c")).reshape(Y * C * rows, block)
    by_z = exchange(jnp.broadcast_to(near[None], (nz, Y * C * rows, block)), "z")
    by_z = by_z.reshape(total, block)

    everywhere = places(counts, jnp.arange(total, dtype=jnp.int32))
    slots = jnp.arange(VALID, dtype=jnp.int32)
    spread = (everywhere[:, None] == slots[None, :]).astype(BF)
    valid = lax.dot_general(spread, by_z, OVER_ROWS, preferred_element_type=F32)
    own = lax.all_gather(valid.astype(BF), "y", axis=0, tiled=False)
    other = swap(own)

    sum_own = gate_up(core, own, gate_weight, up_weight)
    sum_other = gate_up(1 - core, other, gate_weight, up_weight)
    partial = ((sum_own + sum_other) * SCALE).astype(jnp.float16)
    parts = lax.all_gather(partial, "gx", axis=0, tiled=False)
    sums = jnp.sum(parts.astype(F32), axis=0) * (1.0 / SCALE)
    hidden = (jax.nn.silu(sums[:, :hidden_units]) * sums[:, hidden_units:]).astype(BF)

    half = width // C
    w_other = lax.dynamic_slice_in_dim(down_weight, (1 - core) * half, half, 1)
    away = jnp.dot(hidden, w_other, preferred_element_type=F32).astype(BF)
    tile = half // Y * 2 // 3
    pieces = down(core, hidden, down_weight, swap(away), tile)
    column = jnp.sum(exchange(pieces, "y").astype(F32), axis=0).astype(BF)

    first_slot = lax.axis_index("y") % 2 * (VALID // 2)
    spread_half = (everywhere[:, None] == first_slot + slots[None, : VALID // 2]).astype(BF)
    padded = jnp.concatenate(
        (
            jnp.dot(spread, column[:VALID], preferred_element_type=F32).astype(BF),
            jnp.dot(spread_half, column[VALID:], preferred_element_type=F32).astype(BF),
        ),
        axis=1,
    ).reshape(nz, Y * C * rows, 2 * tile)
    summed = jnp.sum(exchange(padded, "z").astype(F32), axis=0).astype(BF)
    mine = exchange(summed.reshape(Y * C, rows, 2 * tile), ("y", "c"))
    mine = mine.reshape(Y, C, rows, 2, tile)
    firsts = mine[:, :, :, 0].transpose(2, 1, 0, 3)
    pairs = mine[:, :, :, 1].reshape(Y // 2, 2, C, rows, tile)
    seconds = (pairs[:, 0] + pairs[:, 1]).transpose(2, 1, 0, 3)
    return jnp.concatenate((firsts, seconds), axis=2).reshape(rows, width)


def solution(mesh):
    gx, yz = mesh.shape["gx"], mesh.shape["yz"]
    fine = Mesh(mesh.devices.reshape(gx, yz // (Y * C), Y, C), ("gx", "z", "y", "c"))
    line = ("z", "y", "c")
    placed = (P(line, "gx"), P(), P("gx", line), P("gx", line), P(line, "gx"))
    return jax.shard_map(
        shards, mesh=fine, in_specs=placed, out_specs=P(line, "gx"), check_vma=False
    )
```

time: 149 us -> 152 us (1.020)
  blocking collectives: 102 us -> 60.2 us
  starting transfers between devices: 13.8 us -> 40.8 us
  waiting for transfers between devices: 22.6 us -> 39.3 us
  matrix products: 4.56 us -> 1.26 us
  Pallas kernels: 0 us -> 3.05 us
    all_to_all x4 -> x2, blocking collectives: 90 us -> 27.4 us  [exchange(): return lax.all_to_all(x, axis, split_axis=0, concat_axis=0, tiled=False)]
    all_to_all x1 -> x3, starting transfers between devices: 3.54 us -> 26.9 us  [exchange(): return lax.all_to_all(x, axis, split_axis=0, concat_axis=0, tiled=False)]
    all_gather x0 -> x1, blocking collectives: none -> 20.8 us  [shards(): own = lax.all_gather(valid.astype(BF), 'y', axis=0, tiled=False)]
    all_to_all x1 -> x3, waiting for transfers between devices: 19.2 us -> 37.7 us  [exchange(): return lax.all_to_all(x, axis, split_axis=0, concat_axis=0, tiled=False)]
    ppermute x2, starting transfers between devices: 10.2 us -> 13.8 us  [swap(): return lax.ppermute(x, 'c', [(0, 1), (1, 0)])]
    dot_general x5 -> x1, matrix products: 3.63 us -> 0.35 us  [shards(): valid = lax.dot_general(spread, by_z, OVER_ROWS, preferred_element_type=F32)]
    pallas_call x0 -> x3, Pallas kernels: none -> 3.05 us  [the longest x2 1.91 us: gate_up(): pl.pallas_call(kernel, out_shape=jax.ShapeDtypeStruct((slots, 2 * units),...]
    ppermute x2, waiting for transfers between devices: 3.39 us -> 1.61 us  [swap(): return lax.ppermute(x, 'c', [(0, 1), (1, 0)])]
  transfers between devices with their start and end apart: 3 -> 5, of which waited for: 3 -> 4; matrix products, arithmetic and copies ran while one was open for 1% -> 1% of each run, Pallas kernels for 0% -> 1%
where the time goes in v3:
time: 152 us; the launch traced here: 151 us
  blocking collectives  60.2 us (40%)
  starting transfers between devices  40.8 us (27%)
  waiting for transfers between devices  39.3 us (26%)
  local copies, waits for them, and re-layouts  4.5 us (3%)
  Pallas kernels  3.05 us (2%)
  other arithmetic  1.98 us (1%)
    all_to_all x3, waiting for transfers between devices, exchange(): return lax.all_to_all(x, axis, split_axis=0, concat_axis=0, tiled=False)  37.7 us
    all_to_all x2, blocking collectives, exchange(): return lax.all_to_all(x, axis, split_axis=0, concat_axis=0, tiled=False)  27.4 us
    all_to_all x3, starting transfers between devices, exchange(): return lax.all_to_all(x, axis, split_axis=0, concat_axis=0, tiled=False)  26.9 us
    all_gather x1, blocking collectives, shards(): own = lax.all_gather(valid.astype(BF), 'y', axis=0, tiled=False)  20.8 us
    ppermute x2, starting transfers between devices, swap(): return lax.ppermute(x, 'c', [(0, 1), (1, 0)])  13.8 us
    all_gather x1, blocking collectives, shards(): parts = lax.all_gather(partial, 'gx', axis=0, tiled=False)  12 us
  transfers between devices with their start and end apart: 5, of which 4 were waited for; matrix products, arithmetic and copies ran while one was open for 1% of the time, Pallas kernels for 1%

profile of v3, /device:TPU:1, one launch (start us, length us, event | category | flops | bytes accessed | tf_op | source)
XLA Modules:
  0.0 151.4 jit_solution(6907960306459550884)
XLA Ops:
  0.0 0.9 reshape.57
  0.9 0.6 copy.41
  1.5 13.8 %all-to-all-start = ((bf16[16,2,192]{2,1,0:T(2,128)(2,1)}), bf16[16,2,192]{2,1,0:T(2,128)(2,1)S(1)}, u32[]{:S(2)}, u32[]{:S(2)}) async-start(bf16[16,2,192]{2,1,0:T(2,128)(2,1)} %bitcast.22), calls=%async_computation | async-start | bytes 32768 | tf_op jit(solution)/shard_map/all_to_all | solution.py:19
  15.3 0.8 select_reduce_fusion.2
  16.1 6.6 %all-to-all-done = bf16[16,2,192]{2,1,0:T(2,128)(2,1)S(1)} async-done(((bf16[16,2,192]{2,1,0:T(2,128)(2,1)}), bf16[16,2,192]{2,1,0:T(2,128)(2,1)S(1)}, u32[]{:S(2)}, u32[]{:S(2)}) %all-to-all-start) | async-done | bytes 12320 | tf_op jit(solution)/shard_map/all_to_all | solution.py:19
  22.8 0.7 broadcast_in_dim.64
  23.5 9.6 %all-to-all-start.1 = ((bf16[12,32,192]{2,1,0:T(8,128)(2,1)}), bf16[12,32,192]{2,1,0:T(8,128)(2,1)S(1)}, u32[]{:S(2)}, u32[]{:S(2)}) async-start(bf16[12,32,192]{2,1,0:T(8,128)(2,1)} %broadcast_in_dim.64), calls=%async_computation.1 | async-start | bytes 393216 | tf_op jit(solution)/shard_map/all_to_all | solution.py:19
  33.1 0.7 select_reduce_fusion.1
  33.9 11.8 %all-to-all-done.1 = bf16[12,32,192]{2,1,0:T(8,128)(2,1)S(1)} async-done(((bf16[12,32,192]{2,1,0:T(8,128)(2,1)}), bf16[12,32,192]{2,1,0:T(8,128)(2,1)S(1)}, u32[]{:S(2)}, u32[]{:S(2)}) %all-to-all-start.1) | async-done | bytes 147488 | tf_op jit(solution)/shard_map/all_to_all | solution.py:19
  45.6 0.3 convolution_convert_fusion.3
  46.0 20.8 %all-gather = bf16[1536,192]{1,0:T(8,128)(2,1)S(1)} all-gather(bf16[192,192]{1,0:T(8,128)(2,1)S(1)} %convolution_convert_fusion.3), channel_id=2, replica_groups=mesh['gx'=4,'z'=12,'y'=8,'c'=2] {'y'}, dimensions={0}, use_global_device_ids=true | all-gather | bytes 663552 | tf_op jit(solution)/shard_map/all_gather | solution.py:131
  66.8 9.5 %collective-permute-start = (bf16[8,192,192]{2,1,0:T(8,128)(2,1)S(1)}, bf16[8,192,192]{2,1,0:T(8,128)(2,1)S(1)}, u32[]{:S(2)}, u32[]{:S(2)}) collective-permute-start(bf16[8,192,192]{2,1,0:T(8,128)(2,1)S(1)} %bitcast.28), channel_id=1, source_target_pairs={{0,1},{1,0},{2,3},{3,2},{4,5},{5,4},{6,7},{7,6},{8,9},{9,8},{10,11... | collective-permute-start | bytes 1769480 | tf_op jit(solution)/shard_map/ppermute | solution.py:23
  76.3 1.4 copy-done.1
  77.7 0.9 shard_map.55
  78.7 1.0 shard_map.56
  79.8 12.0 %all-gather.1 = f16[768,512]{1,0:T(8,128)(2,1)S(1)} all-gather(f16[192,512]{1,0:T(8,128)(2,1)S(1)} %multiply_convert_fusion), channel_id=3, replica_groups=mesh['gx'=4,'z'=12,'y'=8,'c'=2] {'gx'}, dimensions={0}, use_global_device_ids=true | all-gather | bytes 983040 | tf_op jit(solution)/shard_map/all_gather | solution.py:137
  92.4 4.3 %collective-permute-start.1 = (bf16[192,1536]{1,0:T(8,128)(2,1)S(1)}, bf16[192,1536]{1,0:T(8,128)(2,1)S(1)}, u32[]{:S(2)}, u32[]{:S(2)}) collective-permute-start(bf16[192,1536]{1,0:T(8,128)(2,1)S(1)} %convolution_convert_fusion), channel_id=1, source_target_pairs={{0,1},{1,0},{2,3},{3,2},{4,5},{5,4},{6,7},{7,6},{8,9},{9,8},{10,11... | collective-permute-start | bytes 1769480 | tf_op jit(solution)/shard_map/ppermute | solution.py:23
  96.7 1.6 %collective-permute-done.1.got_ref = bf16[192,1536]{1,0:T(8,128)(2,1)S(1)} collective-permute-done((bf16[192,1536]{1,0:T(8,128)(2,1)S(1)}, bf16[192,1536]{1,0:T(8,128)(2,1)S(1)}, u32[]{:S(2)}, u32[]{:S(2)}) %collective-permute-start.1) | collective-permute-done | bytes 589856 | tf_op jit(solution)/shard_map/ppermute | solution.py:23
  98.3 1.1 shard_map.57
  99.4 3.5 %all-to-all-start.2 = ((bf16[8,288,128]{2,1,0:T(8,128)(2,1)}), bf16[8,288,128]{2,1,0:T(8,128)(2,1)S(1)}, u32[]{:S(2)}, u32[]{:S(2)}) async-start(bf16[8,288,128]{2,1,0:T(8,128)(2,1)} %shard_map.57), calls=%async_computation.2 | async-start | bytes 1179648 | tf_op jit(solution)/shard_map/all_to_all | solution.py:19
  103.0 19.3 %all-to-all-done.2 = bf16[8,288,128]{2,1,0:T(8,128)(2,1)S(1)} async-done(((bf16[8,288,128]{2,1,0:T(8,128)(2,1)}), bf16[8,288,128]{2,1,0:T(8,128)(2,1)S(1)}, u32[]{:S(2)}, u32[]{:S(2)}) %all-to-all-start.2) | async-done | bytes 589856 | tf_op jit(solution)/shard_map/all_to_all | solution.py:19
  123.2 15.2 %all_to_all.25 = bf16[12,32,256]{2,1,0:T(8,128)(2,1)S(1)} all-to-all(bf16[12,32,256]{2,1,0:T(8,128)(2,1)S(1)} %bitcast.31), channel_id=1, replica_groups=mesh['gx'=4,'z'=12,'y'=8,'c'=2] {'z'}, dimensions={0} | all-to-all | bytes 393216 | tf_op jit(solution)/shard_map/all_to_all | solution.py:19
  138.4 12.2 %all_to_all.26 = bf16[16,2,256]{2,1,0:T(2,128)(2,1)S(1)} all-to-all(bf16[16,2,256]{2,1,0:T(2,128)(2,1)S(1)} %reshape.62), channel_id=1, replica_groups=mesh['gx'=4,'z'=12,'y'=8,'c'=2] {'y','c'}, dimensions={0} | all-to-all | bytes 32768 | tf_op jit(solution)/shard_map/all_to_all | solution.py:19
  150.8 0.6 reshape.64
  (31 shorter events, 1.7 us)
Async XLA Ops:
  0.0 76.3 %copy-start = (bf16[3072,256]{1,0:T(8,128)(2,1)S(1)}, bf16[3072,256]{1,0:T(8,128)(2,1)}, u32[]{:S(2)}) copy-start(bf16[3072,256]{1,0:T(8,128)(2,1)} %param.7) | copy-start | bytes 4718596
  1.5 21.2 %all-to-all-start = ((bf16[16,2,192]{2,1,0:T(2,128)(2,1)}), bf16[16,2,192]{2,1,0:T(2,128)(2,1)S(1)}, u32[]{:S(2)}, u32[]{:S(2)}) async-start(bf16[16,2,192]{2,1,0:T(2,128)(2,1)} %bitcast.22), calls=%async_computation | async-start | bytes 32768 | tf_op jit(solution)/shard_map/all_to_all | solution.py:19
  23.5 22.2 %all-to-all-start.1 = ((bf16[12,32,192]{2,1,0:T(8,128)(2,1)}), bf16[12,32,192]{2,1,0:T(8,128)(2,1)S(1)}, u32[]{:S(2)}, u32[]{:S(2)}) async-start(bf16[12,32,192]{2,1,0:T(8,128)(2,1)} %broadcast_in_dim.64), calls=%async_computation.1 | async-start | bytes 393216 | tf_op jit(solution)/shard_map/all_to_all | solution.py:19
  66.8 11.9 %collective-permute-start = (bf16[8,192,192]{2,1,0:T(8,128)(2,1)S(1)}, bf16[8,192,192]{2,1,0:T(8,128)(2,1)S(1)}, u32[]{:S(2)}, u32[]{:S(2)}) collective-permute-start(bf16[8,192,192]{2,1,0:T(8,128)(2,1)S(1)} %bitcast.28), channel_id=1, source_target_pairs={{0,1},{1,0},{2,3},{3,2},{4,5},{5,4},{6,7},{7,6},{8,9},{9,8},{10,11... | collective-permute-start | bytes 1769480 | tf_op jit(solution)/shard_map/ppermute | solution.py:23
  76.3 1.4 copy-start.1
  79.8 12.3 %copy-start.2 = (bf16[256,3072]{1,0:T(8,128)(2,1)S(1)}, bf16[256,3072]{1,0:T(8,128)(2,1)}, u32[]{:S(2)}) copy-start(bf16[256,3072]{1,0:T(8,128)(2,1)} %weight_ref.1) | copy-start | bytes 4718596
  92.4 5.9 %collective-permute-start.1 = (bf16[192,1536]{1,0:T(8,128)(2,1)S(1)}, bf16[192,1536]{1,0:T(8,128)(2,1)S(1)}, u32[]{:S(2)}, u32[]{:S(2)}) collective-permute-start(bf16[192,1536]{1,0:T(8,128)(2,1)S(1)} %convolution_convert_fusion), channel_id=1, source_target_pairs={{0,1},{1,0},{2,3},{3,2},{4,5},{5,4},{6,7},{7,6},{8,9},{9,8},{10,11... | collective-permute-start | bytes 1769480 | tf_op jit(solution)/shard_map/ppermute | solution.py:23
  99.4 22.9 %all-to-all-start.2 = ((bf16[8,288,128]{2,1,0:T(8,128)(2,1)}), bf16[8,288,128]{2,1,0:T(8,128)(2,1)S(1)}, u32[]{:S(2)}, u32[]{:S(2)}) async-start(bf16[8,288,128]{2,1,0:T(8,128)(2,1)} %shard_map.57), calls=%async_computation.2 | async-start | bytes 1179648 | tf_op jit(solution)/shard_map/all_to_all | solution.py:19

commit v4 on v1

v4 whole, which is shorter than its diff:
```python
import jax
import jax.numpy as jnp
from jax import lax
from jax.experimental import pallas as pl
from jax.experimental.pallas import tpu as pltpu
from jax.sharding import Mesh, PartitionSpec as P

GROUP_ROWS = 8
VALID = 192
Y = 8
C = 2
BF = jnp.bfloat16
F32 = jnp.float32
SCALE = 32.0
OVER_ROWS = (((0,), (0,)), ((), ()))


def exchange(x, axis):
    return lax.all_to_all(x, axis, split_axis=0, concat_axis=0, tiled=False)


def swap(x):
    return lax.ppermute(x, "c", [(0, 1), (1, 0)])


def places(counts, row_ids):
    n = counts.shape[0]
    before = jnp.sum(
        jnp.where(jnp.arange(n)[None, :] < jnp.arange(n)[:, None], counts[None, :], 0), axis=1
    )
    group = row_ids // GROUP_ROWS
    offset = row_ids - group * GROUP_ROWS
    hits = group[:, None] == jnp.arange(n, dtype=jnp.int32)[None, :]
    start = jnp.sum(jnp.where(hits, before[None, :], 0), axis=1)
    count = jnp.sum(jnp.where(hits, counts[None, :], 0), axis=1)
    return jnp.where(offset < count, start + offset, -1)


def gate_up(kept, pick, other, gate_weight, up_weight):
    slots, width = kept.shape
    units = gate_weight.shape[1]
    steps = 4
    chunk = width // steps

    def kernel(kept_ref, pick_ref, other_ref, gate_ref, up_ref, out_ref):
        x = jnp.dot(pick_ref[...], other_ref[...], preferred_element_type=F32)
        x = (x + kept_ref[...].astype(F32)).astype(BF)
        gate = jnp.dot(x, gate_ref[...], preferred_element_type=F32) * SCALE
        up = jnp.dot(x, up_ref[...], preferred_element_type=F32) * SCALE

        @pl.when(pl.program_id(0) == 0)
        def _():
            out_ref[:, :units] = gate
            out_ref[:, units:] = up

        @pl.when(pl.program_id(0) > 0)
        def _():
            out_ref[:, :units] += gate
            out_ref[:, units:] += up

    def columns(rows):
        return pl.BlockSpec((rows, chunk), lambda i: (0, i))

    weights = pl.BlockSpec((chunk, units), lambda i: (i, 0))
    return pl.pallas_call(
        kernel,
        out_shape=jax.ShapeDtypeStruct((slots, 2 * units), F32),
        grid=(steps,),
        in_specs=[
            columns(slots),
            pl.BlockSpec(pick.shape, lambda i: (0, 0)),
            columns(other.shape[0]),
            weights,
            weights,
        ],
        out_specs=pl.BlockSpec((slots, 2 * units), lambda i: (0, 0)),
        compiler_params=pltpu.CompilerParams(vmem_limit_bytes=16 << 20),
    )(kept, pick, other, gate_weight, up_weight)


def shards(tokens, counts, gate_weight, up_weight, down_weight):
    rows, width = tokens.shape
    hidden_units = gate_weight.shape[1]
    nz = lax.axis_size("z")
    core = lax.axis_index("c")

    by_z = exchange(jnp.broadcast_to(tokens[None], (nz, rows, width)), "z")
    by_z = by_z.reshape(nz * rows, width)
    own = exchange(jnp.broadcast_to(by_z[None], (Y, nz * rows, width)), "y")
    own = own.reshape(Y * nz * rows, width)
    other = swap(own)

    q = jnp.arange(Y * nz * rows, dtype=jnp.int32)
    base = (q // rows % nz) * (Y * C * rows) + (q // (rows * nz)) * (C * rows) + q % rows
    slots = jnp.arange(VALID, dtype=jnp.int32)[:, None]
    pick_own = (slots == places(counts, base + core * rows)[None, :]).astype(BF)
    pick_other = (slots == places(counts, base + (1 - core) * rows)[None, :]).astype(BF)
    kept = jnp.dot(pick_own, own, preferred_element_type=F32).astype(BF)

    partial = gate_up(kept, pick_other, other, gate_weight, up_weight).astype(jnp.float16)
    parts = lax.all_gather(partial, "gx", axis=0, tiled=False)
    sums = jnp.sum(parts.astype(F32), axis=0) * (1.0 / SCALE)
    hidden = (jax.nn.silu(sums[:, :hidden_units]) * sums[:, hidden_units:]).astype(BF)

    mine = lax.dot_general(pick_own, hidden, OVER_ROWS, preferred_element_type=F32).astype(BF)
    theirs = lax.dot_general(pick_other, hidden, OVER_ROWS, preferred_element_type=F32).astype(BF)
    away = jnp.dot(theirs, down_weight, preferred_element_type=F32).astype(BF)
    here = jnp.dot(mine, down_weight, preferred_element_type=F32)
    pair = (here + swap(away).astype(F32)).astype(BF).reshape(Y, nz * rows, width)
    line = jnp.sum(exchange(pair, "y").astype(F32), axis=0).astype(BF).reshape(nz, rows, width)
    return jnp.sum(exchange(line, "z").astype(F32), axis=0).astype(BF)


def solution(mesh):
    gx, yz = mesh.shape["gx"], mesh.shape["yz"]
    fine = Mesh(mesh.devices.reshape(gx, yz // (Y * C), Y, C), ("gx", "z", "y", "c"))
    line = ("z", "y", "c")
    placed = (P(line, "gx"), P(), P("gx", line), P("gx", line), P(line, "gx"))
    return jax.shard_map(
        shards, mesh=fine, in_specs=placed, out_specs=P(line, "gx"), check_vma=False
    )
```

time: 165 us -> 152 us (0.921)
  blocking collectives: 99.2 us -> 88.9 us
  starting transfers between devices: 20.2 us -> 15.1 us
  Pallas kernels: 0 us -> 2.12 us
  other arithmetic: 0.67 us -> 2.73 us
  local copies, waits for them, and re-layouts: 5.43 us -> 3.62 us
    all_to_all x4 -> x3, blocking collectives: 90 us -> 76.9 us  [exchange(): return lax.all_to_all(x, axis, split_axis=0, concat_axis=0, tiled=False)]
    ppermute x2, starting transfers between devices: 12.7 us -> 8.3 us  [swap(): return lax.ppermute(x, 'c', [(0, 1), (1, 0)])]
    all_gather x1, blocking collectives: 9.11 us -> 12 us  [shards(): parts = lax.all_gather(partial, 'gx', axis=0, tiled=False)]
    reshape x4 -> x1, local copies, waits for them, and re-layouts: 2.35 us -> 0.06 us  [shards(): jnp.sum(exchange(pair, 'y').astype(F32), axis=0).astype(BF)]
    pallas_call x0 -> x1, Pallas kernels: none -> 2.12 us  [gate_up(): pl.pallas_call(kernel, out_shape=jax.ShapeDtypeStruct((slots, 2 * units),...]
    reduce_sum x4 -> x3, other arithmetic: 0.29 us -> 2.29 us  [the longest x1 1.45 us: shards(): jnp.sum(exchange(pair, 'y').astype(F32), axis=0).astype(BF)]
    all_to_all x2 -> x1, starting transfers between devices: 7.56 us -> 6.82 us  [exchange(): return lax.all_to_all(x, axis, split_axis=0, concat_axis=0, tiled=False)]
    dot_general x7 -> x3, matrix products: 4.85 us -> 4.34 us  [the longest x1 1.94 us: shards(): here = jnp.dot(mine, down_weight, preferred_element_type=F32)]
  transfers between devices with their start and end apart: 4 -> 3, of which waited for: 4 -> 3; matrix products, arithmetic and copies ran while one was open for 1% -> 1% of each run, Pallas kernels for 0% -> 0%
where the time goes in v4:
time: 152 us; the launch traced here: 150 us
  blocking collectives  88.9 us (58%)
  waiting for transfers between devices  33.5 us (22%)
  starting transfers between devices  15.1 us (10%)
  matrix products  4.34 us (3%)
  local copies, waits for them, and re-layouts  3.62 us (2%)
  other arithmetic  2.73 us (2%)
  Pallas kernels  2.12 us (1%)
    all_to_all x3, blocking collectives, exchange(): return lax.all_to_all(x, axis, split_axis=0, concat_axis=0, tiled=False)  76.9 us
    all_to_all x1, waiting for transfers between devices, exchange(): return lax.all_to_all(x, axis, split_axis=0, concat_axis=0, tiled=False)  30.4 us
    all_gather x1, blocking collectives, shards(): parts = lax.all_gather(partial, 'gx', axis=0, tiled=False)  12 us
    ppermute x2, starting transfers between devices, swap(): return lax.ppermute(x, 'c', [(0, 1), (1, 0)])  8.3 us
    all_to_all x1, starting transfers between devices, exchange(): return lax.all_to_all(x, axis, split_axis=0, concat_axis=0, tiled=False)  6.82 us
    ppermute x2, waiting for transfers between devices, swap(): return lax.ppermute(x, 'c', [(0, 1), (1, 0)])  3.16 us
  transfers between devices with their start and end apart: 3, of which 3 were waited for; matrix products, arithmetic and copies ran while one was open for 1% of the time, Pallas kernels for 0%

profile of v4, /device:TPU:1, one launch (start us, length us, event | category | flops | bytes accessed | tf_op | source)
XLA Modules:
  0.0 150.4 jit_solution(12794337453149917215)
XLA Ops:
  0.0 0.9 broadcast_in_dim.80
  0.9 26.9 %all_to_all.20 = bf16[12,2,3072]{2,1,0:T(2,128)(2,1)S(1)} all-to-all(bf16[12,2,3072]{2,1,0:T(2,128)(2,1)S(1)} %broadcast_in_dim.80), channel_id=1, replica_groups=mesh['gx'=4,'z'=12,'y'=8,'c'=2] {'z'}, dimensions={0} | all-to-all | bytes 294912 | tf_op jit(solution)/shard_map/all_to_all | solution.py:19
  27.8 1.2 broadcast_in_dim.82
  29.0 6.8 %all-to-all-start.1 = ((bf16[8,24,3072]{2,1,0:T(8,128)(2,1)}), bf16[8,24,3072]{2,1,0:T(8,128)(2,1)}, u32[]{:S(2)}, u32[]{:S(2)}) async-start(bf16[8,24,3072]{2,1,0:T(8,128)(2,1)} %broadcast_in_dim.82), calls=%async_computation.1 | async-start | bytes 2359296 | tf_op jit(solution)/shard_map/all_to_all | solution.py:19
  35.9 30.4 %all-to-all-done.1 = bf16[8,24,3072]{2,1,0:T(8,128)(2,1)} async-done(((bf16[8,24,3072]{2,1,0:T(8,128)(2,1)}), bf16[8,24,3072]{2,1,0:T(8,128)(2,1)}, u32[]{:S(2)}, u32[]{:S(2)}) %all-to-all-start.1) | async-done | bytes 1179680 | tf_op jit(solution)/shard_map/all_to_all | solution.py:19
  66.2 4.1 %collective-permute-start = (bf16[192,3072]{1,0:T(8,128)(2,1)}, bf16[192,3072]{1,0:T(8,128)(2,1)S(1)}, u32[]{:S(2)}, u32[]{:S(2)}) collective-permute-start(bf16[192,3072]{1,0:T(8,128)(2,1)} %bitcast), channel_id=1, source_target_pairs={{0,1},{1,0},{2,3},{3,2},{4,5},{5,4},{6,7},{7,6},{8,9},{9,8},{10,11... | collective-permute-start | bytes 3538952 | tf_op jit(solution)/shard_map/ppermute | solution.py:23
  70.4 0.1 select_reduce_fusion.4
  70.5 0.1 select_reduce_fusion.2
  70.7 1.7 %convolution_convert_fusion.1.kept_ref = bf16[192,3072]{1,0:T(8,128)(2,1)S(1)} fusion(bf16[192,3072]{1,0:T(8,128)(2,1)} %bitcast, s32[192]{0:T(256)S(1)} %get-tuple-element.12), kind=kOutput, calls=%fused_computation.1 | convolution fusion | flops 227119104 | bytes 2360064 | tf_op jit(solution)/shard_map/dot_general | solution.py:98
  72.4 0.6 collective-permute-done.other_ref
  73.0 1.4 copy-done.2
  74.4 2.1 %shard_map.55 = f32[192,512]{1,0:T(8,128)S(1)} custom-call(bf16[192,3072]{1,0:T(8,128)(2,1)S(1)} %convolution_convert_fusion.1.kept_ref, bf16[192,192]{1,0:T(8,128)(2,1)S(1)} %fusion.2.pick_ref, bf16[192,3072]{1,0:T(8,128)(2,1)S(1)} %collective-permute-done.other_ref, bf16[3072,256]{1,0:T(8,128)(2,1)S(1)} %copy-done.1, bf16[3072,256]{1,0:T(8,128)(2,1)S(1)} %copy-done.2), custom_call_target="tpu_custom_call" | custom-call | tf_op jit(solution)/shard_map/pallas_call | solution.py:65
  76.6 12.0 %all-gather = f16[768,512]{1,0:T(8,128)(2,1)S(1)} all-gather(f16[192,512]{1,0:T(8,128)(2,1)S(1)} %convert_element_type.37), channel_id=2, replica_groups=mesh['gx'=4,'z'=12,'y'=8,'c'=2] {'gx'}, dimensions={0}, use_global_device_ids=true | all-gather | bytes 983040 | tf_op jit(solution)/shard_map/all_gather | solution.py:101
  88.6 0.1 convert_reduce_fusion
  88.7 0.1 fusion.1
  88.8 0.7 convolution_convert_fusion
  89.5 4.2 %collective-permute-start.1 = (bf16[192,3072]{1,0:T(8,128)(2,1)S(1)}, bf16[192,3072]{1,0:T(8,128)(2,1)}, u32[]{:S(2)}, u32[]{:S(2)}) collective-permute-start(bf16[192,3072]{1,0:T(8,128)(2,1)S(1)} %convolution_convert_fusion), channel_id=1, source_target_pairs={{0,1},{1,0},{2,3},{3,2},{4,5},{5,4},{6,7},{7,6},{8,9},{9,8},{10,11... | collective-permute-start | bytes 3538952 | tf_op jit(solution)/shard_map/ppermute | solution.py:23
  93.7 2.6 %collective-permute-done.1 = bf16[192,3072]{1,0:T(8,128)(2,1)} collective-permute-done((bf16[192,3072]{1,0:T(8,128)(2,1)S(1)}, bf16[192,3072]{1,0:T(8,128)(2,1)}, u32[]{:S(2)}, u32[]{:S(2)}) %collective-permute-start.1) | collective-permute-done | bytes 1179680 | tf_op jit(solution)/shard_map/ppermute | solution.py:23
  96.2 1.9 %add_convert_fusion = bf16[192,3072]{1,0:T(8,128)(2,1)S(1)} fusion(bf16[192,3072]{1,0:T(8,128)(2,1)} %collective-permute-done.1, bf16[256,3072]{1,0:T(8,128)(2,1)S(1)} %copy-done, bf16[192,256]{1,0:T(8,128)(2,1)S(1)} %fusion.1, s32[192]{0:T(256)S(1)} %get-tuple-element.12), kind=kOutput, calls=%fused_computation.2 | convolution fusion | flops 322719744 | bytes 4031232 | tf_op jit(solution)/shard_map/dot_general | solution.py:108
  98.2 35.1 %all_to_all.21 = bf16[8,24,3072]{2,1,0:T(8,128)(2,1)} all-to-all(bf16[8,24,3072]{2,1,0:T(8,128)(2,1)S(1)} %bitcast.9), channel_id=1, replica_groups=mesh['gx'=4,'z'=12,'y'=8,'c'=2] {'y'}, dimensions={0} | all-to-all | bytes 2359296 | tf_op jit(solution)/shard_map/all_to_all | solution.py:19
  133.3 1.4 reduce_sum.88
  134.8 0.1 reshape.177
  134.8 14.9 %all_to_all.22 = bf16[12,2,3072]{2,1,0:T(2,128)(2,1)S(1)} all-to-all(bf16[12,2,3072]{2,1,0:T(2,128)(2,1)S(1)} %reshape.177), channel_id=1, replica_groups=mesh['gx'=4,'z'=12,'y'=8,'c'=2] {'z'}, dimensions={0} | all-to-all | bytes 294912 | tf_op jit(solution)/shard_map/all_to_all | solution.py:19
  149.7 0.7 reduce_sum.89
  (14 shorter events, 0.2 us)
Async XLA Ops:
  0.0 88.8 %copy-start = (bf16[256,3072]{1,0:T(8,128)(2,1)S(1)}, bf16[256,3072]{1,0:T(8,128)(2,1)}, u32[]{:S(2)}) copy-start(bf16[256,3072]{1,0:T(8,128)(2,1)} %param.9) | copy-start | bytes 4718596
  27.8 42.6 %copy-start.3 = (s32[48]{0:T(128)S(1)}, s32[48]{0:T(128)}, u32[]{:S(2)}) copy-start(s32[48]{0:T(128)} %param.6) | copy-start | bytes 580
  29.0 37.2 %all-to-all-start.1 = ((bf16[8,24,3072]{2,1,0:T(8,128)(2,1)}), bf16[8,24,3072]{2,1,0:T(8,128)(2,1)}, u32[]{:S(2)}, u32[]{:S(2)}) async-start(bf16[8,24,3072]{2,1,0:T(8,128)(2,1)} %broadcast_in_dim.82), calls=%async_computation.1 | async-start | bytes 2359296 | tf_op jit(solution)/shard_map/all_to_all | solution.py:19
  35.8 37.2 %copy-start.1 = (bf16[3072,256]{1,0:T(8,128)(2,1)S(1)}, bf16[3072,256]{1,0:T(8,128)(2,1)}, u32[]{:S(2)}) copy-start(bf16[3072,256]{1,0:T(8,128)(2,1)} %gate_ref.1) | copy-start | bytes 4718596
  66.2 6.8 %collective-permute-start = (bf16[192,3072]{1,0:T(8,128)(2,1)}, bf16[192,3072]{1,0:T(8,128)(2,1)S(1)}, u32[]{:S(2)}, u32[]{:S(2)}) collective-permute-start(bf16[192,3072]{1,0:T(8,128)(2,1)} %bitcast), channel_id=1, source_target_pairs={{0,1},{1,0},{2,3},{3,2},{4,5},{5,4},{6,7},{7,6},{8,9},{9,8},{10,11... | collective-permute-start | bytes 3538952 | tf_op jit(solution)/shard_map/ppermute | solution.py:23
  73.0 1.4 copy-start.2
  89.5 6.8 %collective-permute-start.1 = (bf16[192,3072]{1,0:T(8,128)(2,1)S(1)}, bf16[192,3072]{1,0:T(8,128)(2,1)}, u32[]{:S(2)}, u32[]{:S(2)}) collective-permute-start(bf16[192,3072]{1,0:T(8,128)(2,1)S(1)} %convolution_convert_fusion), channel_id=1, source_target_pairs={{0,1},{1,0},{2,3},{3,2},{4,5},{5,4},{6,7},{7,6},{8,9},{9,8},{10,11... | collective-permute-start | bytes 3538952 | tf_op jit(solution)/shard_map/ppermute | solution.py:23

commit v5 on v3

v5 whole, which is shorter than its diff:
```python
import jax
import jax.numpy as jnp
from jax import lax
from jax.experimental import pallas as pl
from jax.experimental.pallas import tpu as pltpu
from jax.sharding import Mesh, PartitionSpec as P

GROUP_ROWS = 8
VALID = 192
Y = 8
C = 2
BF = jnp.bfloat16
F32 = jnp.float32
SCALE = 32.0
OVER_ROWS = (((0,), (0,)), ((), ()))


def exchange(x, axis):
    return lax.all_to_all(x, axis, split_axis=0, concat_axis=0, tiled=False)


def swap(x):
    return lax.ppermute(x, "c", [(0, 1), (1, 0)])


def one_hot(counts_ref, columns, shift):
    shape = (GROUP_ROWS, columns)
    row = lax.broadcasted_iota(jnp.int32, shape, 0)
    ahead = lax.broadcasted_iota(jnp.int32, shape, 1) - row
    start = -shift
    tiles = []
    for group in range(counts_ref.shape[0]):
        count = counts_ref[group]
        tiles.append(jnp.where((ahead == start) & (row < count), 1.0, 0.0))
        start += count
    return jnp.concatenate(tiles, axis=0).astype(BF)


def whole(shape):
    return pl.BlockSpec(shape, lambda *_: (0,) * len(shape))


def cut(tokens):
    rows, width = tokens.shape
    tile = width // (Y * C + Y)

    def kernel(in_ref, out_ref):
        for i in range(Y * C):
            second = Y * C + i // C
            out_ref[i, :, :tile] = in_ref[:, i * tile : (i + 1) * tile]
            out_ref[i, :, tile:] = in_ref[:, second * tile : (second + 1) * tile]

    return pl.pallas_call(
        kernel, out_shape=jax.ShapeDtypeStruct((Y * C, rows, 2 * tile), BF)
    )(tokens)


def compact(core, counts, padded):
    tile = padded.shape[1] // 2
    half = VALID // 2

    def kernel(core_ref, counts_ref, in_ref, out_ref):
        hot = one_hot(counts_ref, VALID, 0)
        x = lax.dot_general(hot, in_ref[...], OVER_ROWS, preferred_element_type=F32).astype(BF)
        first, second = x[:, :tile], x[:, tile:]
        for y in range(Y):
            out_ref[y, :VALID] = first

        @pl.when(core_ref[0] == 0)
        def _():
            for y in range(Y):
                out_ref[y, VALID:] = second[:half]

        @pl.when(core_ref[0] != 0)
        def _():
            for y in range(Y):
                out_ref[y, VALID:] = second[half:]

    shape = (Y, VALID + half, tile)
    return pl.pallas_call(
        kernel,
        out_shape=jax.ShapeDtypeStruct(shape, BF),
        grid_spec=pltpu.PrefetchScalarGridSpec(
            num_scalar_prefetch=2,
            grid=(1,),
            in_specs=[whole(padded.shape)],
            out_specs=whole(shape),
        ),
    )(core[None], counts, padded)


def spread(parity, counts, pieces):
    tile = pieces.shape[2]
    rows = counts.shape[0] * GROUP_ROWS
    half = VALID // 2

    def kernel(parity_ref, counts_ref, in_ref, out_ref):
        total = in_ref[0].astype(F32)
        for y in range(1, Y):
            total += in_ref[y].astype(F32)
        total = total.astype(BF)
        hot = one_hot(counts_ref, VALID, 0)
        hot_half = one_hot(counts_ref, half, parity_ref[0] * half)
        out_ref[:, :tile] = jnp.dot(hot, total[:VALID], preferred_element_type=F32).astype(BF)
        out_ref[:, tile:] = jnp.dot(hot_half, total[VALID:], preferred_element_type=F32).astype(BF)

    return pl.pallas_call(
        kernel,
        out_shape=jax.ShapeDtypeStruct((rows, 2 * tile), BF),
        grid_spec=pltpu.PrefetchScalarGridSpec(
            num_scalar_prefetch=2,
            grid=(1,),
            in_specs=[whole(pieces.shape)],
            out_specs=whole((rows, 2 * tile)),
        ),
    )(parity[None], counts, pieces)


def gate_up(core, own, other, gate_weight, up_weight):
    units = gate_weight.shape[1]
    tile = own.shape[2]
    steps = 3
    chunk = gate_weight.shape[0] // steps

    def kernel(core_ref, own_ref, other_ref, gate_ref, up_ref, out_ref):
        step = pl.program_id(0)
        first = core_ref[0] == 0

        def both(y):
            a, b = own_ref[y], other_ref[y]
            return jnp.where(first, a, b), jnp.where(first, b, a)

        def add(parts, start):
            gate = jnp.zeros((VALID, units), F32)
            up = jnp.zeros((VALID, units), F32)
            for i, x in enumerate(parts):
                depth = pl.ds(i * 2 * tile, 2 * tile)
                gate += jnp.dot(x, gate_ref[depth, :], preferred_element_type=F32)
                up += jnp.dot(x, up_ref[depth, :], preferred_element_type=F32)
            if start:
                out_ref[:, :units] = gate * SCALE
                out_ref[:, units:] = up * SCALE
            else:
                out_ref[:, :units] += gate * SCALE
                out_ref[:, units:] += up * SCALE

        def firsts(start):
            parts = []
            for y in range(start, start + Y // 2):
                a, b = both(y)
                parts.append(jnp.concatenate((a[:VALID], b[:VALID]), axis=1))
            return parts

        def seconds():
            parts = []
            for y in range(0, Y, 2):
                pair = [jnp.concatenate((a[VALID:], b[VALID:]), axis=0) for a, b in (both(y), both(y + 1))]
                parts.append(jnp.concatenate(pair, axis=1))
            return parts

        @pl.when(step == 0)
        def _():
            add(firsts(0), True)

        @pl.when(step == 1)
        def _():
            add(firsts(Y // 2), False)

        @pl.when(step == 2)
        def _():
            add(seconds(), False)

    weights = pl.BlockSpec((chunk, units), lambda i, core: (i, 0))
    return pl.pallas_call(
        kernel,
        out_shape=jax.ShapeDtypeStruct((VALID, 2 * units), F32),
        grid_spec=pltpu.PrefetchScalarGridSpec(
            num_scalar_prefetch=1,
            grid=(steps,),
            in_specs=[whole(own.shape), whole(own.shape), weights, weights],
            out_specs=whole((VALID, 2 * units)),
        ),
        compiler_params=pltpu.CompilerParams(vmem_limit_bytes=24 << 20),
    )(core[None], own, other, gate_weight, up_weight)


def down(core, hidden, down_weight, got, tile):
    slots, units = hidden.shape
    half = got.shape[1]

    def kernel(core_ref, hidden_ref, weight_ref, got_ref, out_ref):
        pair = jnp.dot(hidden_ref[...], weight_ref[...], preferred_element_type=F32)
        pair = (pair + got_ref[...].astype(F32)).astype(BF)
        for i in range(half // tile):
            columns = pair[:, i * tile : (i + 1) * tile]
            if i < Y:
                out_ref[i, :slots] = columns
            else:
                j = 2 * (i - Y)
                out_ref[j, slots:] = columns[: slots // 2]
                out_ref[j + 1, slots:] = columns[slots // 2 :]

    return pl.pallas_call(
        kernel,
        out_shape=jax.ShapeDtypeStruct((Y, slots + slots // 2, tile), BF),
        grid_spec=pltpu.PrefetchScalarGridSpec(
            num_scalar_prefetch=1,
            grid=(1,),
            in_specs=[
                pl.BlockSpec((slots, units), lambda i, core: (0, 0)),
                pl.BlockSpec((units, half), lambda i, core: (0, core[0])),
                pl.BlockSpec((slots, half), lambda i, core: (0, 0)),
            ],
            out_specs=pl.BlockSpec((Y, slots + slots // 2, tile), lambda i, core: (0, 0, 0)),
        ),
        compiler_params=pltpu.CompilerParams(vmem_limit_bytes=16 << 20),
    )(core[None], hidden, down_weight, got)


def join(mine):
    count, rows, block = mine.shape
    tile = block // 2
    tiles = Y + Y // 2

    def kernel(in_ref, out_ref):
        for c in range(C):
            for y in range(Y):
                to = (c * tiles + y) * tile
                out_ref[:, to : to + tile] = in_ref[y * C + c, :, :tile]
            for k in range(Y // 2):
                to = (c * tiles + Y + k) * tile
                a, b = 2 * k * C + c, (2 * k + 1) * C + c
                out_ref[:, to : to + tile] = in_ref[a, :, tile:] + in_ref[b, :, tile:]

    return pl.pallas_call(
        kernel, out_shape=jax.ShapeDtypeStruct((rows, C * tiles * tile), BF)
    )(mine)


def shards(tokens, counts, gate_weight, up_weight, down_weight):
    rows, width = tokens.shape
    hidden_units = gate_weight.shape[1]
    nz = lax.axis_size("z")
    core = lax.axis_index("c")

    near = exchange(cut(tokens), ("y", "c")).reshape(Y * C * rows, -1)
    by_z = exchange(jnp.broadcast_to(near[None], (nz,) + near.shape), "z")

    own = exchange(compact(core, counts, by_z.reshape(nz * Y * C * rows, -1)), "y")
    other = swap(own)

    partial = gate_up(core, own, other, gate_weight, up_weight).astype(jnp.float16)
    parts = lax.all_gather(partial, "gx", axis=0, tiled=False)
    sums = jnp.sum(parts.astype(F32), axis=0) * (1.0 / SCALE)
    hidden = (jax.nn.silu(sums[:, :hidden_units]) * sums[:, hidden_units:]).astype(BF)

    half = width // C
    w_other = lax.dynamic_slice_in_dim(down_weight, (1 - core) * half, half, 1)
    away = jnp.dot(hidden, w_other, preferred_element_type=F32).astype(BF)
    tile = half // Y * 2 // 3
    pieces = down(core, hidden, down_weight, swap(away), tile)

    parity = lax.axis_index("y") % 2
    padded = spread(parity, counts, exchange(pieces, "y")).reshape(nz, Y * C * rows, 2 * tile)
    summed = jnp.sum(exchange(padded, "z").astype(F32), axis=0).astype(BF)
    mine = exchange(summed.reshape(Y * C, rows, 2 * tile), ("y", "c"))
    return join(mine)


def solution(mesh):
    gx, yz = mesh.shape["gx"], mesh.shape["yz"]
    fine = Mesh(mesh.devices.reshape(gx, yz // (Y * C), Y, C), ("gx", "z", "y", "c"))
    line = ("z", "y", "c")
    placed = (P(line, "gx"), P(), P("gx", line), P("gx", line), P(line, "gx"))
    return jax.shard_map(
        shards, mesh=fine, in_specs=placed, out_specs=P(line, "gx"), check_vma=False
    )
```

time: 152 us -> 156 us (1.026)
  blocking collectives: 60.2 us -> 81.9 us
  starting transfers between devices: 40.8 us -> 23.4 us
  Pallas kernels: 3.05 us -> 10.5 us
  waiting for transfers between devices: 39.3 us -> 35.1 us
  other arithmetic: 1.98 us -> 0.27 us
    all_to_all x2 -> x4, blocking collectives: 27.4 us -> 69.8 us  [exchange(): return lax.all_to_all(x, axis, split_axis=0, concat_axis=0, tiled=False)]
    all_gather x1 -> x0, blocking collectives: 20.8 us -> none  [shards(): own = lax.all_gather(valid.astype(BF), 'y', axis=0, tiled=False)]
    all_to_all x3 -> x2, starting transfers between devices: 26.9 us -> 13.2 us  [exchange(): return lax.all_to_all(x, axis, split_axis=0, concat_axis=0, tiled=False)]
    pallas_call x2 -> x5, Pallas kernels: 1.91 us -> 9.35 us  [the longest x1 2.7 us: compact(): pl.pallas_call(kernel, out_shape=jax.ShapeDtypeStruct(shape, BF), grid_sp...]
    all_to_all x3 -> x2, waiting for transfers between devices: 37.7 us -> 31.9 us  [exchange(): return lax.all_to_all(x, axis, split_axis=0, concat_axis=0, tiled=False)]
    ppermute x2, starting transfers between devices: 13.8 us -> 10.2 us  [swap(): return lax.ppermute(x, 'c', [(0, 1), (1, 0)])]
    reshape x4 -> x0, local copies, waits for them, and re-layouts: 2.15 us -> none  [the longest x2 1.52 us: shards(): cut = tokens.reshape(rows, Y * C, block).transpose(1, 0, 2)]
    ppermute x2, waiting for transfers between devices: 1.61 us -> 3.21 us  [swap(): return lax.ppermute(x, 'c', [(0, 1), (1, 0)])]
  transfers between devices with their start and end apart: 5 -> 4, of which waited for: 4 -> 4; matrix products, arithmetic and copies ran while one was open for 1% -> 0% of each run, Pallas kernels for 1% -> 0%
where the time goes in v5:
time: 156 us; the launch traced here: 155 us
  blocking collectives  81.9 us (53%)
  waiting for transfers between devices  35.1 us (22%)
  starting transfers between devices  23.4 us (15%)
  Pallas kernels  10.5 us (7%)
  local copies, waits for them, and re-layouts  3.63 us (2%)
    all_to_all x4, blocking collectives, exchange(): return lax.all_to_all(x, axis, split_axis=0, concat_axis=0, tiled=False)  69.8 us
    all_to_all x2, waiting for transfers between devices, exchange(): return lax.all_to_all(x, axis, split_axis=0, concat_axis=0, tiled=False)  31.9 us
    all_to_all x2, starting transfers between devices, exchange(): return lax.all_to_all(x, axis, split_axis=0, concat_axis=0, tiled=False)  13.2 us
    all_gather x1, blocking collectives, shards(): parts = lax.all_gather(partial, 'gx', axis=0, tiled=False)  12.1 us
    ppermute x2, starting transfers between devices, swap(): return lax.ppermute(x, 'c', [(0, 1), (1, 0)])  10.2 us
    ppermute x2, waiting for transfers between devices, swap(): return lax.ppermute(x, 'c', [(0, 1), (1, 0)])  3.21 us
  transfers between devices with their start and end apart: 4, of which 4 were waited for; matrix products, arithmetic and copies ran while one was open for 0% of the time, Pallas kernels for 0%

profile of v5, /device:TPU:1, one launch (start us, length us, event | category | flops | bytes accessed | tf_op | source)
XLA Modules:
  0.0 155.2 jit_solution(12975609081099211402)
XLA Ops:
  0.0 1.4 shard_map.55
  1.4 21.2 %all_to_all.30 = bf16[16,2,256]{2,1,0:T(2,128)(2,1)S(1)} all-to-all(bf16[16,2,256]{2,1,0:T(2,128)(2,1)} %shard_map.55), channel_id=1, replica_groups=mesh['gx'=4,'z'=12,'y'=8,'c'=2] {'y','c'}, dimensions={0} | all-to-all | bytes 32768 | tf_op jit(solution)/shard_map/all_to_all | solution.py:19
  22.6 0.7 broadcast_in_dim.18
  23.3 9.6 %all-to-all-start.1 = ((bf16[12,32,256]{2,1,0:T(8,128)(2,1)}), bf16[12,32,256]{2,1,0:T(8,128)(2,1)S(1)}, u32[]{:S(2)}, u32[]{:S(2)}) async-start(bf16[12,32,256]{2,1,0:T(8,128)(2,1)} %broadcast_in_dim.18), calls=%async_computation.1 | async-start | bytes 393216 | tf_op jit(solution)/shard_map/all_to_all | solution.py:19
  33.0 12.5 %all-to-all-done.1 = bf16[12,32,256]{2,1,0:T(8,128)(2,1)S(1)} async-done(((bf16[12,32,256]{2,1,0:T(8,128)(2,1)}), bf16[12,32,256]{2,1,0:T(8,128)(2,1)S(1)}, u32[]{:S(2)}, u32[]{:S(2)}) %all-to-all-start.1) | async-done | bytes 196640 | tf_op jit(solution)/shard_map/all_to_all | solution.py:19
  45.5 0.7 copy-done.4
  46.2 2.7 %shard_map.56 = bf16[8,288,128]{2,1,0:T(8,128)(2,1)} custom-call(s32[1]{0:T(128)} %bitcast.1.core_ref, s32[48]{0:T(128)} %counts_ref.3, bf16[384,256]{1,0:T(8,128)(2,1)} %bitcast.8), custom_call_target="tpu_custom_call" | custom-call | tf_op jit(solution)/shard_map/pallas_call | solution.py:80
  48.9 19.2 %all_to_all.31.own_ref = bf16[8,288,128]{2,1,0:T(8,128)(2,1)S(1)} all-to-all(bf16[8,288,128]{2,1,0:T(8,128)(2,1)} %shard_map.56), channel_id=1, replica_groups=mesh['gx'=4,'z'=12,'y'=8,'c'=2] {'y'}, dimensions={0} | all-to-all | bytes 1179648 | tf_op jit(solution)/shard_map/all_to_all | solution.py:19
  68.0 6.0 %collective-permute-start = (bf16[8,288,128]{2,1,0:T(8,128)(2,1)S(1)}, bf16[8,288,128]{2,1,0:T(8,128)(2,1)S(1)}, u32[]{:S(2)}, u32[]{:S(2)}) collective-permute-start(bf16[8,288,128]{2,1,0:T(8,128)(2,1)S(1)} %all_to_all.31.own_ref), channel_id=1, source_target_pairs={{0,1},{1,0},{2,3},{3,2},{4,5},{5,4},{6,7},{7,6},{8,9},{9,8},{10,11... | collective-permute-start | bytes 1769480 | tf_op jit(solution)/shard_map/ppermute | solution.py:23
  74.1 1.6 %collective-permute-done.other_ref = bf16[8,288,128]{2,1,0:T(8,128)(2,1)S(1)} collective-permute-done((bf16[8,288,128]{2,1,0:T(8,128)(2,1)S(1)}, bf16[8,288,128]{2,1,0:T(8,128)(2,1)S(1)}, u32[]{:S(2)}, u32[]{:S(2)}) %collective-permute-start) | collective-permute-done | bytes 589856 | tf_op jit(solution)/shard_map/ppermute | solution.py:23
  75.7 1.4 copy-done.2
  77.1 1.2 shard_map.57
  78.3 12.1 %all-gather = f16[768,512]{1,0:T(8,128)(2,1)S(1)} all-gather(f16[192,512]{1,0:T(8,128)(2,1)S(1)} %convert_element_type.14), channel_id=2, replica_groups=mesh['gx'=4,'z'=12,'y'=8,'c'=2] {'gx'}, dimensions={0}, use_global_device_ids=true | all-gather | bytes 983040 | tf_op jit(solution)/shard_map/all_gather | solution.py:253
  90.7 0.3 convolution_convert_fusion
  91.0 4.2 %collective-permute-start.1 = (bf16[192,1536]{1,0:T(8,128)(2,1)S(1)}, bf16[192,1536]{1,0:T(8,128)(2,1)S(1)}, u32[]{:S(2)}, u32[]{:S(2)}) collective-permute-start(bf16[192,1536]{1,0:T(8,128)(2,1)S(1)} %convolution_convert_fusion), channel_id=1, source_target_pairs={{0,1},{1,0},{2,3},{3,2},{4,5},{5,4},{6,7},{7,6},{8,9},{9,8},{10,11... | collective-permute-start | bytes 1769480 | tf_op jit(solution)/shard_map/ppermute | solution.py:23
  95.2 1.6 %collective-permute-done.1.got_ref = bf16[192,1536]{1,0:T(8,128)(2,1)S(1)} collective-permute-done((bf16[192,1536]{1,0:T(8,128)(2,1)S(1)}, bf16[192,1536]{1,0:T(8,128)(2,1)S(1)}, u32[]{:S(2)}, u32[]{:S(2)}) %collective-permute-start.1) | collective-permute-done | bytes 589856 | tf_op jit(solution)/shard_map/ppermute | solution.py:23
  96.8 1.2 shard_map.58
  98.0 3.5 %all-to-all-start.3 = ((bf16[8,288,128]{2,1,0:T(8,128)(2,1)}), bf16[8,288,128]{2,1,0:T(8,128)(2,1)S(1)}, u32[]{:S(2)}, u32[]{:S(2)}) async-start(bf16[8,288,128]{2,1,0:T(8,128)(2,1)} %shard_map.58), calls=%async_computation.3 | async-start | bytes 1179648 | tf_op jit(solution)/shard_map/all_to_all | solution.py:19
  101.5 19.3 %all-to-all-done.3.in_ref = bf16[8,288,128]{2,1,0:T(8,128)(2,1)S(1)} async-done(((bf16[8,288,128]{2,1,0:T(8,128)(2,1)}), bf16[8,288,128]{2,1,0:T(8,128)(2,1)S(1)}, u32[]{:S(2)}, u32[]{:S(2)}) %all-to-all-start.3) | async-done | bytes 589856 | tf_op jit(solution)/shard_map/all_to_all | solution.py:19
  120.9 0.8 copy-done.3
  121.7 2.7 %shard_map.59 = bf16[384,256]{1,0:T(8,128)(2,1)} custom-call(s32[1]{0:T(128)} %bitcast.parity_ref, s32[48]{0:T(128)} %counts_ref.3, bf16[8,288,128]{2,1,0:T(8,128)(2,1)} %copy-done.3), custom_call_target="tpu_custom_call" | custom-call | tf_op jit(solution)/shard_map/pallas_call | solution.py:107
  124.4 16.5 %all_to_all.32 = bf16[12,32,256]{2,1,0:T(8,128)(2,1)S(1)} all-to-all(bf16[12,32,256]{2,1,0:T(8,128)(2,1)} %bitcast.9), channel_id=1, replica_groups=mesh['gx'=4,'z'=12,'y'=8,'c'=2] {'z'}, dimensions={0} | all-to-all | bytes 393216 | tf_op jit(solution)/shard_map/all_to_all | solution.py:19
  141.0 12.9 %all_to_all.33.in_ref = bf16[16,2,256]{2,1,0:T(2,128)(2,1)} all-to-all(bf16[16,2,256]{2,1,0:T(2,128)(2,1)S(1)} %reshape.12), channel_id=1, replica_groups=mesh['gx'=4,'z'=12,'y'=8,'c'=2] {'y','c'}, dimensions={0} | all-to-all | bytes 32768 | tf_op jit(solution)/shard_map/all_to_all | solution.py:19
  153.9 1.3 shard_map.60
  (14 shorter events, 0.3 us)
Async XLA Ops:
  0.0 75.7 %copy-start.1 = (bf16[3072,256]{1,0:T(8,128)(2,1)S(1)}, bf16[3072,256]{1,0:T(8,128)(2,1)}, u32[]{:S(2)}) copy-start(bf16[3072,256]{1,0:T(8,128)(2,1)} %gate_ref.1) | copy-start | bytes 4718596
  23.3 22.2 %all-to-all-start.1 = ((bf16[12,32,256]{2,1,0:T(8,128)(2,1)}), bf16[12,32,256]{2,1,0:T(8,128)(2,1)S(1)}, u32[]{:S(2)}, u32[]{:S(2)}) async-start(bf16[12,32,256]{2,1,0:T(8,128)(2,1)} %broadcast_in_dim.18), calls=%async_computation.1 | async-start | bytes 393216 | tf_op jit(solution)/shard_map/all_to_all | solution.py:19
  45.5 0.7 copy-start.4
  68.0 7.6 %collective-permute-start = (bf16[8,288,128]{2,1,0:T(8,128)(2,1)S(1)}, bf16[8,288,128]{2,1,0:T(8,128)(2,1)S(1)}, u32[]{:S(2)}, u32[]{:S(2)}) collective-permute-start(bf16[8,288,128]{2,1,0:T(8,128)(2,1)S(1)} %all_to_all.31.own_ref), channel_id=1, source_target_pairs={{0,1},{1,0},{2,3},{3,2},{4,5},{5,4},{6,7},{7,6},{8,9},{9,8},{10,11... | collective-permute-start | bytes 1769480 | tf_op jit(solution)/shard_map/ppermute | solution.py:23
  75.7 1.4 copy-start.2
  78.3 12.4 %copy-start = (bf16[256,3072]{1,0:T(8,128)(2,1)S(1)}, bf16[256,3072]{1,0:T(8,128)(2,1)}, u32[]{:S(2)}) copy-start(bf16[256,3072]{1,0:T(8,128)(2,1)} %weight_ref.1) | copy-start | bytes 4718596
  91.0 5.8 %collective-permute-start.1 = (bf16[192,1536]{1,0:T(8,128)(2,1)S(1)}, bf16[192,1536]{1,0:T(8,128)(2,1)S(1)}, u32[]{:S(2)}, u32[]{:S(2)}) collective-permute-start(bf16[192,1536]{1,0:T(8,128)(2,1)S(1)} %convolution_convert_fusion), channel_id=1, source_target_pairs={{0,1},{1,0},{2,3},{3,2},{4,5},{5,4},{6,7},{7,6},{8,9},{9,8},{10,11... | collective-permute-start | bytes 1769480 | tf_op jit(solution)/shard_map/ppermute | solution.py:23
  98.0 22.9 %all-to-all-start.3 = ((bf16[8,288,128]{2,1,0:T(8,128)(2,1)}), bf16[8,288,128]{2,1,0:T(8,128)(2,1)S(1)}, u32[]{:S(2)}, u32[]{:S(2)}) async-start(bf16[8,288,128]{2,1,0:T(8,128)(2,1)} %shard_map.58), calls=%async_computation.3 | async-start | bytes 1179648 | tf_op jit(solution)/shard_map/all_to_all | solution.py:19
  120.9 0.8 copy-start.3

commit v6 on v5

--- a/solution.py
+++ b/solution.py
@@ -23,97 +23,8 @@
     return lax.ppermute(x, "c", [(0, 1), (1, 0)])
 
 
-def one_hot(counts_ref, columns, shift):
-    shape = (GROUP_ROWS, columns)
-    row = lax.broadcasted_iota(jnp.int32, shape, 0)
-    ahead = lax.broadcasted_iota(jnp.int32, shape, 1) - row
-    start = -shift
-    tiles = []
-    for group in range(counts_ref.shape[0]):
-        count = counts_ref[group]
-        tiles.append(jnp.where((ahead == start) & (row < count), 1.0, 0.0))
-        start += count
-    return jnp.concatenate(tiles, axis=0).astype(BF)
-
-
 def whole(shape):
     return pl.BlockSpec(shape, lambda *_: (0,) * len(shape))
-
-
-def cut(tokens):
-    rows, width = tokens.shape
-    tile = width // (Y * C + Y)
-
-    def kernel(in_ref, out_ref):
-        for i in range(Y * C):
-            second = Y * C + i // C
-            out_ref[i, :, :tile] = in_ref[:, i * tile : (i + 1) * tile]
-            out_ref[i, :, tile:] = in_ref[:, second * tile : (second + 1) * tile]
-
-    return pl.pallas_call(
-        kernel, out_shape=jax.ShapeDtypeStruct((Y * C, rows, 2 * tile), BF)
-    )(tokens)
-
-
-def compact(core, counts, padded):
-    tile = padded.shape[1] // 2
-    half = VALID // 2
-
-    def kernel(core_ref, counts_ref, in_ref, out_ref):
-        hot = one_hot(counts_ref, VALID, 0)
-        x = lax.dot_general(hot, in_ref[...], OVER_ROWS, preferred_element_type=F32).astype(BF)
-        first, second = x[:, :tile], x[:, tile:]
-        for y in range(Y):
-            out_ref[y, :VALID] = first
-
-        @pl.when(core_ref[0] == 0)
-        def _():
-            for y in range(Y):
-                out_ref[y, VALID:] = second[:half]
-
-        @pl.when(core_ref[0] != 0)
-        def _():
-            for y in range(Y):
-                out_ref[y, VALID:] = second[half:]
-
-    shape = (Y, VALID + half, tile)
-    return pl.pallas_call(
-        kernel,
-        out_shape=jax.ShapeDtypeStruct(shape, BF),
-        grid_spec=pltpu.PrefetchScalarGridSpec(
-            num_scalar_prefetch=2,
-            grid=(1,),
-            in_specs=[whole(padded.shape)],
-            out_specs=whole(shape),
-        ),
-    )(core[None], counts, padded)
-
-
-def spread(parity, counts, pieces):
-    tile = pieces.shape[2]
-    rows = counts.shape[0] * GROUP_ROWS
-    half = VALID // 2
-
-    def kernel(parity_ref, counts_ref, in_ref, out_ref):
-        total = in_ref[0].astype(F32)
-        for y in range(1, Y):
-            total += in_ref[y].astype(F32)
-        total = total.astype(BF)
-        hot = one_hot(counts_ref, VALID, 0)
-        hot_half = one_hot(counts_ref, half, parity_ref[0] * half)
-        out_ref[:, :tile] = jnp.dot(hot, total[:VALID], preferred_element_type=F32).astype(BF)
-        out_ref[:, tile:] = jnp.dot(hot_half, total[VALID:], preferred_element_type=F32).astype(BF)
-
-    return pl.pallas_call(
-        kernel,
-        out_shape=jax.ShapeDtypeStruct((rows, 2 * tile), BF),
-        grid_spec=pltpu.PrefetchScalarGridSpec(
-            num_scalar_prefetch=2,
-            grid=(1,),
-            in_specs=[whole(pieces.shape)],
-            out_specs=whole((rows, 2 * tile)),
-        ),
-    )(parity[None], counts, pieces)
 
 
 def gate_up(core, own, other, gate_weight, up_weight):
@@ -217,36 +128,48 @@
     )(core[None], hidden, down_weight, got)
 
 
-def join(mine):
-    count, rows, block = mine.shape
-    tile = block // 2
-    tiles = Y + Y // 2
-
-    def kernel(in_ref, out_ref):
-        for c in range(C):
-            for y in range(Y):
-                to = (c * tiles + y) * tile
-                out_ref[:, to : to + tile] = in_ref[y * C + c, :, :tile]
-            for k in range(Y // 2):
-                to = (c * tiles + Y + k) * tile
-                a, b = 2 * k * C + c, (2 * k + 1) * C + c
-                out_ref[:, to : to + tile] = in_ref[a, :, tile:] + in_ref[b, :, tile:]
-
-    return pl.pallas_call(
-        kernel, out_shape=jax.ShapeDtypeStruct((rows, C * tiles * tile), BF)
-    )(mine)
+def one_hot(starts, ends, columns, shift):
+    shape = (starts.shape[0], GROUP_ROWS, columns)
+    row = lax.broadcasted_iota(jnp.int32, shape, 1)
+    place = lax.broadcasted_iota(jnp.int32, shape, 2) + shift
+    hit = (place - row == starts[:, None, None]) & (place < ends[:, None, None])
+    return hit.astype(BF).reshape(-1, columns)
 
 
 def shards(tokens, counts, gate_weight, up_weight, down_weight):
     rows, width = tokens.shape
     hidden_units = gate_weight.shape[1]
     nz = lax.axis_size("z")
+    near = Y * C * rows
+    tile = width // (Y * C + Y)
+    half_rows = VALID // 2
+
     core = lax.axis_index("c")
-
-    near = exchange(cut(tokens), ("y", "c")).reshape(Y * C * rows, -1)
-    by_z = exchange(jnp.broadcast_to(near[None], (nz,) + near.shape), "z")
-
-    own = exchange(compact(core, counts, by_z.reshape(nz * Y * C * rows, -1)), "y")
+    shift = lax.axis_index("y") % 2 * half_rows
+    w_start = (1 - core) * (width // C)
+    half_start = core * half_rows
+    groups = jnp.arange(counts.shape[0], dtype=jnp.int32)
+    starts = jnp.sum(jnp.where(groups[None, :] < groups[:, None], counts[None, :], 0), axis=1)
+    ends = jnp.sum(jnp.where(groups[None, :] <= groups[:, None], counts[None, :], 0), axis=1)
+    hot = one_hot(starts, ends, VALID, 0)
+    hot_half = one_hot(starts, ends, half_rows, shift)
+    tokens, hot, hot_half, core, w_start, half_start = lax.optimization_barrier(
+        (tokens, hot, hot_half, core, w_start, half_start)
+    )
+
+    tiles = tokens.reshape(rows, width // tile, tile).transpose(1, 0, 2)
+    seconds = jnp.repeat(tiles[Y * C :], C, axis=0)
+    cut = jnp.stack((tiles[: Y * C], seconds), axis=1)
+    got = exchange(cut, ("y", "c")).transpose(0, 2, 1, 3).reshape(near, 2 * tile)
+    by_z = exchange(jnp.broadcast_to(got[None], (nz,) + got.shape), "z")
+    by_z = by_z.reshape(nz * near, 2 * tile)
+
+    valid = lax.dot_general(hot, by_z, OVER_ROWS, preferred_element_type=F32).astype(BF)
+    second = lax.dynamic_slice(
+        valid, (half_start, tile), (half_rows, tile), allow_negative_indices=False
+    )
+    block = jnp.concatenate((valid[:, :tile], second), axis=0)
+    own = exchange(jnp.broadcast_to(block[None], (Y,) + block.shape), "y")
     other = swap(own)
 
     partial = gate_up(core, own, other, gate_weight, up_weight).astype(jnp.float16)
@@ -254,17 +177,28 @@
     sums = jnp.sum(parts.astype(F32), axis=0) * (1.0 / SCALE)
     hidden = (jax.nn.silu(sums[:, :hidden_units]) * sums[:, hidden_units:]).astype(BF)
 
-    half = width // C
-    w_other = lax.dynamic_slice_in_dim(down_weight, (1 - core) * half, half, 1)
+    w_other = lax.dynamic_slice(
+        down_weight, (0, w_start), (hidden_units, width // C), allow_negative_indices=False
+    )
     away = jnp.dot(hidden, w_other, preferred_element_type=F32).astype(BF)
-    tile = half // Y * 2 // 3
     pieces = down(core, hidden, down_weight, swap(away), tile)
-
-    parity = lax.axis_index("y") % 2
-    padded = spread(parity, counts, exchange(pieces, "y")).reshape(nz, Y * C * rows, 2 * tile)
+    column = jnp.sum(exchange(pieces, "y").astype(F32), axis=0).astype(BF)
+
+    padded = jnp.concatenate(
+        (
+            jnp.dot(hot, column[:VALID], preferred_element_type=F32).astype(BF),
+            jnp.dot(hot_half, column[VALID:], preferred_element_type=F32).astype(BF),
+        ),
+        axis=1,
+    ).reshape(nz, near, 2 * tile)
     summed = jnp.sum(exchange(padded, "z").astype(F32), axis=0).astype(BF)
-    mine = exchange(summed.reshape(Y * C, rows, 2 * tile), ("y", "c"))
-    return join(mine)
+    home = summed.reshape(Y * C, rows, 2, tile).transpose(0, 2, 1, 3)
+    mine = exchange(home, ("y", "c")).reshape(Y, C, 2, rows, tile)
+    firsts = mine[:, :, 0].transpose(1, 0, 2, 3)
+    pairs = mine[:, :, 1].reshape(Y // 2, 2, C, rows, tile)
+    seconds = (pairs[:, 0] + pairs[:, 1]).transpose(1, 0, 2, 3)
+    out = jnp.concatenate((firsts, seconds), axis=1).reshape(width // tile, rows, tile)
+    return out.transpose(1, 0, 2).reshape(rows, width)
 
 
 def solution(mesh):

time: 156 us -> 144 us (0.923)
  blocking collectives: 81.9 us -> 124 us
  waiting for transfers between devices: 35.1 us -> 3.22 us
  starting transfers between devices: 23.4 us -> 10.2 us
  Pallas kernels: 10.5 us -> 1.52 us
    all_to_all x4 -> x6, blocking collectives: 69.8 us -> 112 us  [exchange(): return lax.all_to_all(x, axis, split_axis=0, concat_axis=0, tiled=False)]
    all_to_all x2 -> x0, waiting for transfers between devices: 31.9 us -> none  [exchange(): return lax.all_to_all(x, axis, split_axis=0, concat_axis=0, tiled=False)]
    all_to_all x2 -> x0, starting transfers between devices: 13.2 us -> none  [exchange(): return lax.all_to_all(x, axis, split_axis=0, concat_axis=0, tiled=False)]
    pallas_call x4 -> x0, Pallas kernels: 8.15 us -> none  [the longest x1 2.7 us: compact(): pl.pallas_call(kernel, out_shape=jax.ShapeDtypeStruct(shape, BF), grid_sp...]
    unnamed x10 -> x8, local copies, waits for them, and re-layouts: 2.91 us -> 0.74 us
  transfers between devices with their start and end apart: 4 -> 2, of which waited for: 4 -> 2; matrix products, arithmetic and copies ran while one was open for 0% -> 0% of each run, Pallas kernels for 0% -> 0%
where the time goes in v6:
time: 144 us
  blocking collectives  124 us (86%)
  starting transfers between devices  10.2 us (7%)
  waiting for transfers between devices  3.22 us (2%)
  local copies, waits for them, and re-layouts  2.14 us (1%)
  other arithmetic  1.63 us (1%)
  Pallas kernels  1.52 us (1%)
    all_to_all x6, blocking collectives, exchange(): return lax.all_to_all(x, axis, split_axis=0, concat_axis=0, tiled=False)  112 us
    all_gather x1, blocking collectives, shards(): parts = lax.all_gather(partial, 'gx', axis=0, tiled=False)  12.1 us
    ppermute x2, starting transfers between devices, swap(): return lax.ppermute(x, 'c', [(0, 1), (1, 0)])  10.2 us
    ppermute x2, waiting for transfers between devices, swap(): return lax.ppermute(x, 'c', [(0, 1), (1, 0)])  3.22 us
  transfers between devices with their start and end apart: 2, of which 2 were waited for; matrix products, arithmetic and copies ran while one was open for 0% of the time, Pallas kernels for 0%

profile of v6, /device:TPU:1, one launch (start us, length us, event | category | flops | bytes accessed | tf_op | source)
XLA Modules:
  0.0 144.0 jit_solution(11513868288226746793)
XLA Ops:
  0.0 0.8 select_reduce_fusion.1
  1.2 0.2 fusion.2
  1.4 0.2 fusion.5
  1.7 0.7 copy.46
  2.4 20.3 %all_to_all.30 = bf16[16,2,2,128]{3,2,1,0:T(2,128)(2,1)S(1)} all-to-all(bf16[16,2,2,128]{3,2,1,0:T(2,128)(2,1)S(1)} %copy.27), channel_id=1, replica_groups=mesh['gx'=4,'z'=12,'y'=8,'c'=2] {'y','c'}, dimensions={0} | all-to-all | bytes 32768 | tf_op jit(solution)/shard_map/all_to_all | solution.py:19
  22.8 22.9 %all_to_all.31 = bf16[12,32,256]{2,1,0:T(8,128)(2,1)S(1)} all-to-all(bf16[12,32,256]{2,1,0:T(8,128)(2,1)S(1)} %broadcast_in_dim.51), channel_id=1, replica_groups=mesh['gx'=4,'z'=12,'y'=8,'c'=2] {'z'}, dimensions={0} | all-to-all | bytes 393216 | tf_op jit(solution)/shard_map/all_to_all | solution.py:19
  45.8 0.2 convolution_convert_fusion.2
  46.2 18.1 %all_to_all.32.own_ref = bf16[8,288,128]{2,1,0:T(8,128)(2,1)S(1)} all-to-all(bf16[8,288,128]{2,1,0:T(8,128)(2,1)S(1)} %broadcast_in_dim.52), channel_id=1, replica_groups=mesh['gx'=4,'z'=12,'y'=8,'c'=2] {'y'}, dimensions={0} | all-to-all | bytes 1179648 | tf_op jit(solution)/shard_map/all_to_all | solution.py:19
  64.3 6.0 %collective-permute-start = (bf16[8,288,128]{2,1,0:T(8,128)(2,1)S(1)}, bf16[8,288,128]{2,1,0:T(8,128)(2,1)S(1)}, u32[]{:S(2)}, u32[]{:S(2)}) collective-permute-start(bf16[8,288,128]{2,1,0:T(8,128)(2,1)S(1)} %all_to_all.32.own_ref), channel_id=1, source_target_pairs={{0,1},{1,0},{2,3},{3,2},{4,5},{5,4},{6,7},{7,6},{8,9},{9,8},{10,11... | collective-permute-start | bytes 1769480 | tf_op jit(solution)/shard_map/ppermute | solution.py:23
  70.3 1.6 %collective-permute-done.other_ref = bf16[8,288,128]{2,1,0:T(8,128)(2,1)S(1)} collective-permute-done((bf16[8,288,128]{2,1,0:T(8,128)(2,1)S(1)}, bf16[8,288,128]{2,1,0:T(8,128)(2,1)S(1)}, u32[]{:S(2)}, u32[]{:S(2)}) %collective-permute-start) | collective-permute-done | bytes 589856 | tf_op jit(solution)/shard_map/ppermute | solution.py:23
  71.9 1.2 shard_map.55
  73.2 12.1 %all-gather = f16[768,512]{1,0:T(8,128)(2,1)S(1)} all-gather(f16[192,512]{1,0:T(8,128)(2,1)S(1)} %convert_element_type.36), channel_id=2, replica_groups=mesh['gx'=4,'z'=12,'y'=8,'c'=2] {'gx'}, dimensions={0}, use_global_device_ids=true | all-gather | bytes 983040 | tf_op jit(solution)/shard_map/all_gather | solution.py:176
  85.3 0.1 convert_reduce_fusion
  85.5 0.5 convolution_convert_fusion
  86.0 4.2 %collective-permute-start.1 = (bf16[192,1536]{1,0:T(8,128)(2,1)S(1)}, bf16[192,1536]{1,0:T(8,128)(2,1)S(1)}, u32[]{:S(2)}, u32[]{:S(2)}) collective-permute-start(bf16[192,1536]{1,0:T(8,128)(2,1)S(1)} %convolution_convert_fusion), channel_id=1, source_target_pairs={{0,1},{1,0},{2,3},{3,2},{4,5},{5,4},{6,7},{7,6},{8,9},{9,8},{10,11... | collective-permute-start | bytes 1769480 | tf_op jit(solution)/shard_map/ppermute | solution.py:23
  90.2 1.6 %collective-permute-done.1.got_ref = bf16[192,1536]{1,0:T(8,128)(2,1)S(1)} collective-permute-done((bf16[192,1536]{1,0:T(8,128)(2,1)S(1)}, bf16[192,1536]{1,0:T(8,128)(2,1)S(1)}, u32[]{:S(2)}, u32[]{:S(2)}) %collective-permute-start.1) | collective-permute-done | bytes 589856 | tf_op jit(solution)/shard_map/ppermute | solution.py:23
  91.8 0.3 shard_map.56
  92.1 21.8 %all_to_all.33 = bf16[8,288,128]{2,1,0:T(8,128)(2,1)S(1)} all-to-all(bf16[8,288,128]{2,1,0:T(8,128)(2,1)S(1)} %shard_map.56), channel_id=1, replica_groups=mesh['gx'=4,'z'=12,'y'=8,'c'=2] {'y'}, dimensions={0} | all-to-all | bytes 1179648 | tf_op jit(solution)/shard_map/all_to_all | solution.py:19
  114.0 0.2 convolution_convert_fusion.3
  114.2 0.2 convolution_convert_fusion.1
  114.5 0.1 copy.29
  114.6 16.4 %all_to_all.34 = bf16[12,32,256]{2,1,0:T(8,128)(2,1)S(1)} all-to-all(bf16[12,32,256]{2,1,0:T(8,128)(2,1)S(1)} %bitcast.43), channel_id=1, replica_groups=mesh['gx'=4,'z'=12,'y'=8,'c'=2] {'z'}, dimensions={0} | all-to-all | bytes 393216 | tf_op jit(solution)/shard_map/all_to_all | solution.py:19
  131.1 12.2 %all_to_all.35 = bf16[16,2,2,128]{3,1,2,0:T(2,128)(2,1)S(1)} all-to-all(bf16[16,2,2,128]{3,1,2,0:T(2,128)(2,1)S(1)} %bitcast.49), channel_id=1, replica_groups=mesh['gx'=4,'z'=12,'y'=8,'c'=2] {'y','c'}, dimensions={0} | all-to-all | bytes 32768 | tf_op jit(solution)/shard_map/all_to_all | solution.py:19
  143.4 0.6 copy.34
  (38 shorter events, 1.0 us)
Async XLA Ops:
  22.8 49.1 %copy-start.1 = (bf16[3072,256]{1,0:T(8,128)(2,1)S(1)}, bf16[3072,256]{1,0:T(8,128)(2,1)}, u32[]{:S(2)}) copy-start(bf16[3072,256]{1,0:T(8,128)(2,1)} %gate_ref.1) | copy-start | bytes 4718596
  22.8 49.1 %copy-start.2 = (bf16[3072,256]{1,0:T(8,128)(2,1)S(1)}, bf16[3072,256]{1,0:T(8,128)(2,1)}, u32[]{:S(2)}) copy-start(bf16[3072,256]{1,0:T(8,128)(2,1)} %up_ref.1) | copy-start | bytes 4718596
  64.3 7.6 %collective-permute-start = (bf16[8,288,128]{2,1,0:T(8,128)(2,1)S(1)}, bf16[8,288,128]{2,1,0:T(8,128)(2,1)S(1)}, u32[]{:S(2)}, u32[]{:S(2)}) collective-permute-start(bf16[8,288,128]{2,1,0:T(8,128)(2,1)S(1)} %all_to_all.32.own_ref), channel_id=1, source_target_pairs={{0,1},{1,0},{2,3},{3,2},{4,5},{5,4},{6,7},{7,6},{8,9},{9,8},{10,11... | collective-permute-start | bytes 1769480 | tf_op jit(solution)/shard_map/ppermute | solution.py:23
  73.1 12.4 %copy-start = (bf16[256,3072]{1,0:T(8,128)(2,1)S(1)}, bf16[256,3072]{1,0:T(8,128)(2,1)}, u32[]{:S(2)}) copy-start(bf16[256,3072]{1,0:T(8,128)(2,1)} %weight_ref.1) | copy-start | bytes 4718596
  86.0 5.8 %collective-permute-start.1 = (bf16[192,1536]{1,0:T(8,128)(2,1)S(1)}, bf16[192,1536]{1,0:T(8,128)(2,1)S(1)}, u32[]{:S(2)}, u32[]{:S(2)}) collective-permute-start(bf16[192,1536]{1,0:T(8,128)(2,1)S(1)} %convolution_convert_fusion), channel_id=1, source_target_pairs={{0,1},{1,0},{2,3},{3,2},{4,5},{5,4},{6,7},{7,6},{8,9},{9,8},{10,11... | collective-permute-start | bytes 1769480 | tf_op jit(solution)/shard_map/ppermute | solution.py:23

commit v7 on v6

--- a/solution.py
+++ b/solution.py
@@ -153,14 +153,15 @@
     ends = jnp.sum(jnp.where(groups[None, :] <= groups[:, None], counts[None, :], 0), axis=1)
     hot = one_hot(starts, ends, VALID, 0)
     hot_half = one_hot(starts, ends, half_rows, shift)
-    tokens, hot, hot_half, core, w_start, half_start = lax.optimization_barrier(
-        (tokens, hot, hot_half, core, w_start, half_start)
-    )
 
     tiles = tokens.reshape(rows, width // tile, tile).transpose(1, 0, 2)
     seconds = jnp.repeat(tiles[Y * C :], C, axis=0)
     cut = jnp.stack((tiles[: Y * C], seconds), axis=1)
-    got = exchange(cut, ("y", "c")).transpose(0, 2, 1, 3).reshape(near, 2 * tile)
+    got = exchange(cut, ("y", "c"))
+    got, hot, hot_half, core, w_start, half_start = lax.optimization_barrier(
+        (got, hot, hot_half, core, w_start, half_start)
+    )
+    got = got.transpose(0, 2, 1, 3).reshape(near, 2 * tile)
     by_z = exchange(jnp.broadcast_to(got[None], (nz,) + got.shape), "z")
     by_z = by_z.reshape(nz * near, 2 * tile)
 

time: 144 us -> 144 us (level)
  blocking collectives: 124 us -> 103 us
  starting transfers between devices: 10.2 us -> 24 us
  waiting for transfers between devices: 3.22 us -> 8.94 us
    all_to_all x6 -> x5, blocking collectives: 112 us -> 90.7 us  [exchange(): return lax.all_to_all(x, axis, split_axis=0, concat_axis=0, tiled=False)]
    all_to_all x0 -> x1, starting transfers between devices: none -> 13.8 us  [exchange(): return lax.all_to_all(x, axis, split_axis=0, concat_axis=0, tiled=False)]
    all_to_all x0 -> x1, waiting for transfers between devices: none -> 5.73 us  [exchange(): return lax.all_to_all(x, axis, split_axis=0, concat_axis=0, tiled=False)]
  transfers between devices with their start and end apart: 2 -> 3, of which waited for: 2 -> 3; matrix products, arithmetic and copies ran while one was open for 0% -> 1% of each run, Pallas kernels for 0% -> 0%
where the time goes in v7:
time: 144 us; the launch traced here: 143 us
  blocking collectives  103 us (72%)
  starting transfers between devices  24 us (17%)
  waiting for transfers between devices  8.94 us (6%)
  local copies, waits for them, and re-layouts  2.73 us (2%)
  other arithmetic  1.63 us (1%)
  Pallas kernels  1.52 us (1%)
    all_to_all x5, blocking collectives, exchange(): return lax.all_to_all(x, axis, split_axis=0, concat_axis=0, tiled=False)  90.7 us
    all_to_all x1, starting transfers between devices, exchange(): return lax.all_to_all(x, axis, split_axis=0, concat_axis=0, tiled=False)  13.8 us
    all_gather x1, blocking collectives, shards(): parts = lax.all_gather(partial, 'gx', axis=0, tiled=False)  12.1 us
    ppermute x2, starting transfers between devices, swap(): return lax.ppermute(x, 'c', [(0, 1), (1, 0)])  10.2 us
    all_to_all x1, waiting for transfers between devices, exchange(): return lax.all_to_all(x, axis, split_axis=0, concat_axis=0, tiled=False)  5.73 us
    ppermute x2, waiting for transfers between devices, swap(): return lax.ppermute(x, 'c', [(0, 1), (1, 0)])  3.22 us
  transfers between devices with their start and end apart: 3, of which 3 were waited for; matrix products, arithmetic and copies ran while one was open for 1% of the time, Pallas kernels for 0%

profile of v7, /device:TPU:1, one launch (start us, length us, event | category | flops | bytes accessed | tf_op | source)
XLA Modules:
  0.0 143.1 jit_solution(7379213367640551638)
XLA Ops:
  0.0 0.7 copy.46
  0.7 0.6 copy.27
  1.3 13.8 %all-to-all-start = ((bf16[16,2,2,128]{3,2,1,0:T(2,128)(2,1)}), bf16[16,2,2,128]{3,2,1,0:T(2,128)(2,1)S(1)}, u32[]{:S(2)}, u32[]{:S(2)}) async-start(bf16[16,2,2,128]{3,2,1,0:T(2,128)(2,1)} %copy.27), calls=%async_computation | async-start | bytes 32768 | tf_op jit(solution)/shard_map/all_to_all | solution.py:19
  15.2 0.8 select_reduce_fusion.1
  16.4 0.2 fusion.2
  16.6 0.2 fusion.5
  16.8 5.7 %all-to-all-done = bf16[16,2,2,128]{3,2,1,0:T(2,128)(2,1)S(1)} async-done(((bf16[16,2,2,128]{3,2,1,0:T(2,128)(2,1)}), bf16[16,2,2,128]{3,2,1,0:T(2,128)(2,1)S(1)}, u32[]{:S(2)}, u32[]{:S(2)}) %all-to-all-start) | async-done | bytes 16416 | tf_op jit(solution)/shard_map/all_to_all | solution.py:19
  22.6 22.2 %all_to_all.30 = bf16[12,32,256]{2,1,0:T(8,128)(2,1)S(1)} all-to-all(bf16[12,32,256]{2,1,0:T(8,128)(2,1)S(1)} %broadcast_in_dim.51), channel_id=1, replica_groups=mesh['gx'=4,'z'=12,'y'=8,'c'=2] {'z'}, dimensions={0} | all-to-all | bytes 393216 | tf_op jit(solution)/shard_map/all_to_all | solution.py:19
  44.9 0.2 convolution_convert_fusion.2
  45.3 18.1 %all_to_all.31.own_ref = bf16[8,288,128]{2,1,0:T(8,128)(2,1)S(1)} all-to-all(bf16[8,288,128]{2,1,0:T(8,128)(2,1)S(1)} %broadcast_in_dim.52), channel_id=1, replica_groups=mesh['gx'=4,'z'=12,'y'=8,'c'=2] {'y'}, dimensions={0} | all-to-all | bytes 1179648 | tf_op jit(solution)/shard_map/all_to_all | solution.py:19
  63.4 6.0 %collective-permute-start = (bf16[8,288,128]{2,1,0:T(8,128)(2,1)S(1)}, bf16[8,288,128]{2,1,0:T(8,128)(2,1)S(1)}, u32[]{:S(2)}, u32[]{:S(2)}) collective-permute-start(bf16[8,288,128]{2,1,0:T(8,128)(2,1)S(1)} %all_to_all.31.own_ref), channel_id=1, source_target_pairs={{0,1},{1,0},{2,3},{3,2},{4,5},{5,4},{6,7},{7,6},{8,9},{9,8},{10,11... | collective-permute-start | bytes 1769480 | tf_op jit(solution)/shard_map/ppermute | solution.py:23
  69.4 1.6 %collective-permute-done.other_ref = bf16[8,288,128]{2,1,0:T(8,128)(2,1)S(1)} collective-permute-done((bf16[8,288,128]{2,1,0:T(8,128)(2,1)S(1)}, bf16[8,288,128]{2,1,0:T(8,128)(2,1)S(1)}, u32[]{:S(2)}, u32[]{:S(2)}) %collective-permute-start) | collective-permute-done | bytes 589856 | tf_op jit(solution)/shard_map/ppermute | solution.py:23
  71.0 1.2 shard_map.55
  72.3 12.1 %all-gather = f16[768,512]{1,0:T(8,128)(2,1)S(1)} all-gather(f16[192,512]{1,0:T(8,128)(2,1)S(1)} %convert_element_type.36), channel_id=2, replica_groups=mesh['gx'=4,'z'=12,'y'=8,'c'=2] {'gx'}, dimensions={0}, use_global_device_ids=true | all-gather | bytes 983040 | tf_op jit(solution)/shard_map/all_gather | solution.py:177
  84.6 0.5 convolution_convert_fusion
  85.1 4.2 %collective-permute-start.1 = (bf16[192,1536]{1,0:T(8,128)(2,1)S(1)}, bf16[192,1536]{1,0:T(8,128)(2,1)S(1)}, u32[]{:S(2)}, u32[]{:S(2)}) collective-permute-start(bf16[192,1536]{1,0:T(8,128)(2,1)S(1)} %convolution_convert_fusion), channel_id=1, source_target_pairs={{0,1},{1,0},{2,3},{3,2},{4,5},{5,4},{6,7},{7,6},{8,9},{9,8},{10,11... | collective-permute-start | bytes 1769480 | tf_op jit(solution)/shard_map/ppermute | solution.py:23
  89.3 1.6 %collective-permute-done.1.got_ref = bf16[192,1536]{1,0:T(8,128)(2,1)S(1)} collective-permute-done((bf16[192,1536]{1,0:T(8,128)(2,1)S(1)}, bf16[192,1536]{1,0:T(8,128)(2,1)S(1)}, u32[]{:S(2)}, u32[]{:S(2)}) %collective-permute-start.1) | collective-permute-done | bytes 589856 | tf_op jit(solution)/shard_map/ppermute | solution.py:23
  90.9 0.3 shard_map.56
  91.2 21.8 %all_to_all.32 = bf16[8,288,128]{2,1,0:T(8,128)(2,1)S(1)} all-to-all(bf16[8,288,128]{2,1,0:T(8,128)(2,1)S(1)} %shard_map.56), channel_id=1, replica_groups=mesh['gx'=4,'z'=12,'y'=8,'c'=2] {'y'}, dimensions={0} | all-to-all | bytes 1179648 | tf_op jit(solution)/shard_map/all_to_all | solution.py:19
  113.1 0.2 convolution_convert_fusion.3
  113.3 0.2 convolution_convert_fusion.1
  113.7 16.4 %all_to_all.33 = bf16[12,32,256]{2,1,0:T(8,128)(2,1)S(1)} all-to-all(bf16[12,32,256]{2,1,0:T(8,128)(2,1)S(1)} %bitcast.43), channel_id=1, replica_groups=mesh['gx'=4,'z'=12,'y'=8,'c'=2] {'z'}, dimensions={0} | all-to-all | bytes 393216 | tf_op jit(solution)/shard_map/all_to_all | solution.py:19
  130.2 12.2 %all_to_all.34 = bf16[16,2,2,128]{3,1,2,0:T(2,128)(2,1)S(1)} all-to-all(bf16[16,2,2,128]{3,1,2,0:T(2,128)(2,1)S(1)} %bitcast.49), channel_id=1, replica_groups=mesh['gx'=4,'z'=12,'y'=8,'c'=2] {'y','c'}, dimensions={0} | all-to-all | bytes 32768 | tf_op jit(solution)/shard_map/all_to_all | solution.py:19
  142.5 0.6 copy.34
  (39 shorter events, 1.2 us)
Async XLA Ops:
  1.3 21.2 %all-to-all-start = ((bf16[16,2,2,128]{3,2,1,0:T(2,128)(2,1)}), bf16[16,2,2,128]{3,2,1,0:T(2,128)(2,1)S(1)}, u32[]{:S(2)}, u32[]{:S(2)}) async-start(bf16[16,2,2,128]{3,2,1,0:T(2,128)(2,1)} %copy.27), calls=%async_computation | async-start | bytes 32768 | tf_op jit(solution)/shard_map/all_to_all | solution.py:19
  22.6 48.4 %copy-start.1 = (bf16[3072,256]{1,0:T(8,128)(2,1)S(1)}, bf16[3072,256]{1,0:T(8,128)(2,1)}, u32[]{:S(2)}) copy-start(bf16[3072,256]{1,0:T(8,128)(2,1)} %gate_ref.1) | copy-start | bytes 4718596
  22.6 48.4 %copy-start.2 = (bf16[3072,256]{1,0:T(8,128)(2,1)S(1)}, bf16[3072,256]{1,0:T(8,128)(2,1)}, u32[]{:S(2)}) copy-start(bf16[3072,256]{1,0:T(8,128)(2,1)} %up_ref.1) | copy-start | bytes 4718596
  63.4 7.6 %collective-permute-start = (bf16[8,288,128]{2,1,0:T(8,128)(2,1)S(1)}, bf16[8,288,128]{2,1,0:T(8,128)(2,1)S(1)}, u32[]{:S(2)}, u32[]{:S(2)}) collective-permute-start(bf16[8,288,128]{2,1,0:T(8,128)(2,1)S(1)} %all_to_all.31.own_ref), channel_id=1, source_target_pairs={{0,1},{1,0},{2,3},{3,2},{4,5},{5,4},{6,7},{7,6},{8,9},{9,8},{10,11... | collective-permute-start | bytes 1769480 | tf_op jit(solution)/shard_map/ppermute | solution.py:23
  72.3 12.4 %copy-start = (bf16[256,3072]{1,0:T(8,128)(2,1)S(1)}, bf16[256,3072]{1,0:T(8,128)(2,1)}, u32[]{:S(2)}) copy-start(bf16[256,3072]{1,0:T(8,128)(2,1)} %weight_ref.1) | copy-start | bytes 4718596
  85.1 5.8 %collective-permute-start.1 = (bf16[192,1536]{1,0:T(8,128)(2,1)S(1)}, bf16[192,1536]{1,0:T(8,128)(2,1)S(1)}, u32[]{:S(2)}, u32[]{:S(2)}) collective-permute-start(bf16[192,1536]{1,0:T(8,128)(2,1)S(1)} %convolution_convert_fusion), channel_id=1, source_target_pairs={{0,1},{1,0},{2,3},{3,2},{4,5},{5,4},{6,7},{7,6},{8,9},{9,8},{10,11... | collective-permute-start | bytes 1769480 | tf_op jit(solution)/shard_map/ppermute | solution.py:23
